TPU v7x, 32 devices: a whole 2x2x4 slice. The times are simulated.
32 devices in a mesh: group: 4 (over x, core), resp: 8 (over z, y).
Axes of the slice: x: 2, y: 2, z: 4, core: 2. Of those that a mesh axis runs over, the one named last changes fastest.
Arguments:
- prompt_in: bfloat16 [4, 1024, 10240], P('group', 'resp'), may hold values from -6 to 6
- prompt_dt: bfloat16 [4, 1024, 128], P('group', 'resp'), may hold values from -3 to 9
- doc_starts: int32 [4, 4], P('group'), may hold values from 0 to 127, as said below
- resp_in: bfloat16 [4, 8, 256, 10240], P('group', 'resp'), may hold values from -6 to 6
- resp_dt: bfloat16 [4, 8, 256, 128], P('group', 'resp'), may hold values from -3 to 9
- resp_len: int32 [4, 8], P('group', 'resp'), may hold values from 64 to 256, as said below
- upstream: bfloat16 [4, 8, 256, 8192], P('group', 'resp'), may hold values from -6 to 6
- reward: float32 [4, 8], P('group', 'resp'), may hold values from -4 to 4
- conv_w: float32 [4, 10240], replicated, may hold values from -3 to 3
- conv_b: float32 [10240], replicated, may hold values from -0.5 to 0.5
- head_params: float32 [3, 128], replicated, may hold values from -5.5 to 1.5
Outputs:
- grad_conv_w: float32 [4, 10240], replicated
- grad_conv_b: float32 [10240], replicated
- grad_heads: float32 [3, 128], replicated
Inputs may be any that keep to these rules, and one draw needn't show every extreme that they name: doc_starts begins with 0 and rises strictly; all documents but the last start within the first 128 positions. `resp_len`: each group has a response of 256 tokens.
All inputs are finite; a program needn't handle non-finite values.
Results may differ from a plain program's by a relative error of at most 0.01.
Values may be sent and summed in bfloat16 or wider, within the bound.
No kernel may reach another device: no remote copies, remote signals or barrier semaphores. Data moves between devices by JAX's collectives and lax.ppermute only.
A program may use at most 448 MiB of HBM per device.

v0:
```python
import jax
import jax.numpy as jnp
from jax import lax
from jax.sharding import PartitionSpec as P

H = 128
P_SIZE = 64
N = 256
G = 4
K = 4


def passed_along(block, axis, distance):
    devices = range(lax.axis_size(axis))
    route = [(i - distance, i) for i in devices if i - distance in devices]
    return lax.ppermute(block, axis, route)


def prefix(shard, axis, combine, identity):
    devices, here = (lax.axis_size(axis), lax.axis_index(axis))
    everything = jax.tree.map(
        lambda part, kind: lax.all_gather(part.astype(kind), axis),
        shard,
        (jnp.bfloat16, jnp.bfloat16),
    )
    start = jax.tree.map(
        lambda part, zero: jnp.broadcast_to(jnp.asarray(zero, part.dtype), part.shape),
        shard,
        identity,
    )

    def prefix_lap(k, before):
        reached = k < here
        new = combine(
            before, jax.tree.map(lambda part, own: part[k].astype(own.dtype), everything, shard)
        )
        return jax.tree.map(lambda a, b: jnp.where(reached, a, b), new, before)

    return lax.fori_loop(0, devices, prefix_lap, start)


def from_root(block, axis, owner):
    block = jnp.where(lax.axis_index(axis) == owner, block, jnp.zeros_like(block))
    return lax.psum(block, axis)


def carried_in(shard, axis, combine, identity):
    devices, here = (lax.axis_size(axis), lax.axis_index(axis))
    everything = lax.all_gather(shard, axis)
    start = jnp.broadcast_to(jnp.asarray(identity, shard.dtype), shard.shape)

    def carried_lap(k, before):
        at = devices - 1 - k
        reached = at > here
        new = combine(before, everything[at])
        return jnp.where(reached, new, before)

    return lax.fori_loop(0, devices, carried_lap, start)


def doc_number(starts, positions):
    return jnp.sum((starts[None, :] <= positions[:, None]).astype(jnp.int32), axis=1)


def conv_silu(inputs_rows, conv_tail, tap_mask, conv_w, conv_b):
    n_rows = inputs_rows.shape[0]
    taps_back = conv_w.shape[0] - 1
    extended = jnp.concatenate([conv_tail, inputs_rows], axis=0).astype(jnp.float32)
    total = conv_b[None, :] + conv_w[taps_back][None, :] * extended[taps_back:]
    for offset in range(1, taps_back + 1):
        total = (
            total
            + conv_w[taps_back - offset][None, :]
            * extended[taps_back - offset : taps_back - offset + n_rows]
            * tap_mask[:, offset - 1 : offset]
        )
    return jax.nn.silu(total).astype(jnp.bfloat16)


def prompt_state(params, inputs_rows, step_unbounded, conv_tail, tap_mask, in_last, carry_on):
    conv_w, conv_b, head_params = params
    n_rows = inputs_rows.shape[0]
    activated = conv_silu(inputs_rows, conv_tail, tap_mask, conv_w, conv_b)
    x_part = activated[:, : H * P_SIZE].reshape(n_rows, G, H // G, P_SIZE)
    b_part = activated[:, H * P_SIZE : H * P_SIZE + G * N].reshape(n_rows, G, N)
    step_size = jax.nn.softplus(step_unbounded.astype(jnp.float32) + head_params[1][None, :])
    log_decay = -jnp.exp(head_params[0])[None, :] * step_size
    whole_log = jnp.sum(log_decay, axis=0)
    after_log = whole_log[None, :] - jnp.cumsum(log_decay, axis=0)
    weighting = in_last[:, None] * jnp.exp(after_log) * step_size
    scaled = (x_part * weighting.reshape(n_rows, G, H // G, 1)).astype(jnp.bfloat16)
    ssm_state = jnp.einsum(
        "tgjp,tgn->gjpn", scaled, b_part, preferred_element_type=jnp.float32
    ).reshape(H, P_SIZE, N)
    return (ssm_state, carry_on * jnp.exp(whole_log))


def group_mix(inputs):
    c_part, b_part, x_part, step_size, cum_decay, begin = inputs
    n_rows = c_part.shape[0]
    scores = jnp.dot(c_part, b_part.T, preferred_element_type=jnp.float32)
    log_gap = cum_decay.T[:, :, None] - cum_decay.T[:, None, :]
    causal = jnp.arange(n_rows)[:, None] >= jnp.arange(n_rows)[None, :]
    decays = jnp.exp(jnp.where(causal[None], log_gap, -1e30))
    weights_mix = (scores[None] * decays * step_size.T[:, None, :]).astype(jnp.bfloat16)
    within = jnp.einsum("jts,sjp->tjp", weights_mix, x_part, preferred_element_type=jnp.float32)
    carried = (
        jnp.einsum("tn,jpn->tjp", c_part, begin, preferred_element_type=jnp.float32)
        * jnp.exp(cum_decay)[:, :, None]
    )
    return within + carried


def response_out(params, begin, inputs_rows, step_unbounded, conv_tail):
    conv_w, conv_b, head_params = params
    n_rows = inputs_rows.shape[0]
    per_group = H // G
    activated = conv_silu(
        inputs_rows, conv_tail, jnp.ones((n_rows, K - 1), jnp.float32), conv_w, conv_b
    )
    x_part = activated[:, : H * P_SIZE].reshape(n_rows, G, per_group, P_SIZE)
    b_part = activated[:, H * P_SIZE : H * P_SIZE + G * N].reshape(n_rows, G, N)
    c_part = activated[:, H * P_SIZE + G * N :].reshape(n_rows, G, N)
    step_size = jax.nn.softplus(step_unbounded.astype(jnp.float32) + head_params[1][None, :])
    cum_decay = jnp.cumsum(-jnp.exp(head_params[0])[None, :] * step_size, axis=0)
    mixed = lax.map(
        jax.checkpoint(group_mix),
        (
            c_part.transpose(1, 0, 2),
            b_part.transpose(1, 0, 2),
            x_part.transpose(1, 0, 2, 3),
            step_size.reshape(n_rows, G, per_group).transpose(1, 0, 2),
            cum_decay.reshape(n_rows, G, per_group).transpose(1, 0, 2),
            begin.reshape(G, per_group, P_SIZE, N),
        ),
    )
    flat = mixed.transpose(1, 0, 2, 3).reshape(n_rows, H * P_SIZE)
    return (
        flat
        + x_part.reshape(n_rows, H * P_SIZE).astype(jnp.float32)
        * jnp.repeat(head_params[2], P_SIZE)[None, :]
    )


def combine_states(earlier, later_pair):
    return (earlier[0] * later_pair[0], later_pair[0][:, None, None] * earlier[1] + later_pair[1])


def multiply(earlier, later_pair):
    return earlier * later_pair


def shards(
    prompt_in,
    prompt_dt,
    doc_starts,
    resp_in,
    resp_dt,
    resp_len,
    upstream,
    reward,
    conv_w,
    conv_b,
    head_params,
):
    params = (conv_w, conv_b, head_params)
    n_ranks = lax.axis_size("resp")
    my_rank = lax.axis_index("resp")
    block_rows = prompt_in.shape[1]
    taps_back = conv_w.shape[0] - 1
    prompt_rows = prompt_in[0]
    starts = doc_starts[0]
    positions = my_rank * block_rows + jnp.arange(block_rows, dtype=jnp.int32)
    doc_ids = doc_number(starts, positions)
    tap_mask = jnp.stack(
        [
            (doc_number(starts, positions - offset) == doc_ids).astype(jnp.float32)
            for offset in range(1, taps_back + 1)
        ],
        axis=1,
    )
    last_doc = doc_ids[block_rows - 1]
    in_last = (doc_ids == last_doc).astype(jnp.float32)
    carry_on = (doc_number(starts, positions[:1] - 1)[0] == last_doc).astype(jnp.float32)
    local_tail_rows = prompt_rows[block_rows - taps_back :]
    prev_tail = passed_along(local_tail_rows, "resp", 1)

    def local_prompt(prm):
        return prompt_state(prm, prompt_rows, prompt_dt[0], prev_tail, tap_mask, in_last, carry_on)

    (ssm_state, decay_total), prompt_pull = jax.vjp(local_prompt, params)
    identity = (jnp.ones((H,), jnp.float32), jnp.zeros((H, P_SIZE, N), jnp.float32))
    _, before_state = prefix((decay_total, ssm_state), "resp", combine_states, identity)
    through = decay_total[:, None, None] * before_state + ssm_state
    start, conv_tail = (
        from_root(through.astype(jnp.bfloat16), "resp", n_ranks - 1),
        from_root(local_tail_rows, "resp", n_ranks - 1),
    )
    suffix_decay = carried_in(decay_total, "resp", multiply, jnp.ones((H,), jnp.float32))
    total_reward = lax.psum(reward[0, 0], "resp")
    advantage = reward[0, 0] - total_reward / n_ranks
    slots = resp_in.shape[2]
    in_length = (jnp.arange(slots) < resp_len[0, 0]).astype(jnp.float32)
    cotangent = upstream[0, 0].astype(jnp.float32) * (advantage / slots * in_length)[:, None]

    def respond(prm, begin):
        return response_out(prm, begin, resp_in[0, 0], resp_dt[0, 0], conv_tail)

    _, resp_pull = jax.vjp(respond, params, start)
    resp_grads, begin_grad = resp_pull(cotangent)
    grad_state = lax.psum(begin_grad, "resp").astype(jnp.float32)
    prompt_grads = prompt_pull(
        (
            suffix_decay[:, None, None] * grad_state,
            suffix_decay * jnp.sum(grad_state * before_state, axis=(1, 2)),
        )
    )[0]
    return lax.psum(
        (
            resp_grads[0] + prompt_grads[0],
            resp_grads[1] + prompt_grads[1],
            resp_grads[2] + prompt_grads[2],
        ),
        ("group", "resp"),
    )


def solution(mesh):
    in_specs = (
        P("group", "resp", None),
        P("group", "resp", None),
        P("group", None),
        P("group", "resp", None, None),
        P("group", "resp", None, None),
        P("group", "resp"),
        P("group", "resp", None, None),
        P("group", "resp"),
        P(),
        P(),
        P(),
    )
    out_specs = (P(), P(), P())
    return jax.shard_map(shards, mesh=mesh, in_specs=in_specs, out_specs=out_specs, check_vma=False)
```

profile of v0, /device:TPU:0, one launch (start us, length us, event | category | flops | bytes accessed | tf_op | source)
XLA Modules:
  0.0 1434.3 jit_solution(17859425528690306502)
XLA Ops:
  7.2 3.2 copy.100
  12.5 2.2 copy.106
  14.7 4.9 collective-permute-start
  24.0 3.3 maximum_convert_fusion.1
  27.4 14.1 multiply_convert_fusion.10
  41.7 5.8 fusion.102
  47.6 63.7 %psum.51 = f32[]{:T(128)} all-reduce(f32[]{:T(128)} %bitcast.61), channel_id=1, replica_groups=mesh['group'=4,'resp'=8] {'resp'}, use_global_device_ids=true, to_apply=%region_0.0 | all-reduce | flops 1 | bytes 8 | tf_op jit(solution)/shard_map/psum | solution.py:200
  115.4 25.0 %all-gather.2 = bf16[8,1,128]{2,1,0:T(2,128)(2,1)S(1)} all-gather(bf16[1,1,128]{2,1,0:T(2,128)(2,1)S(1)} %get-tuple-element.678), channel_id=3, replica_groups=mesh['group'=4,'resp'=8] {'resp'}, dimensions={0}, use_global_device_ids=true | all-gather | bytes 2304 | tf_op jit(solution)/shard_map/all_gather | solution.py:22
  140.8 8.0 copy.101
  150.7 246.5 %psum.49 = bf16[3,10240]{0,1:T(8,128)(2,1)S(1)} all-reduce(bf16[3,10240]{0,1:T(8,128)(2,1)} %broadcast_select_fusion.2), channel_id=1, replica_groups=mesh['group'=4,'resp'=8] {'resp'}, use_global_device_ids=true, to_apply=%region_1.0 | all-reduce | flops 30720 | bytes 122880 | tf_op jit(solution)/shard_map/psum | solution.py:44
  397.3 9.2 maximum_convert_fusion
  406.5 28.0 %multiply_convert_fusion.8 = (bf16[256,10240]{0,1:T(8,128)(2,1)}, f32[256,10240]{0,1:T(8,128)}) fusion(f32[259,10240]{0,1:T(8,128)} %maximum_convert_fusion, f32[10240]{0:T(1024)S(1)} %bitcast.395, f32[10240]{0:T(1024)S(1)} %bitcast.397, f32[10240]{0:T(1024)S(1)} %bitcast.393, f32[10240]{0:T(1024)S(1)} %bitcast.391, f32[10240]{0:T(1024)S(1)} %copy-done.20), kind=kLoop, calls=%fused_computation.76 | loop fusion | flops 34078720 | bytes 57876480 | tf_op jit(solution)/shard_map/jvp()/convert_element_type | solution.py:77
  434.5 351.5 %all-gather.6.cloned.1.call-done = bf16[8,128,64,256]{3,2,1,0:T(8,128)(2,1)} async-done(((bf16[1,128,64,256]{3,2,1,0:T(8,128)(2,1)}), bf16[8,128,64,256]{3,2,1,0:T(8,128)(2,1)}) %all-gather.6.cloned.1.call-update) | async-done | bytes 33554448 | tf_op jit(solution)/shard_map/all_gather | solution.py:22
  786.0 61.5 %while.55 = (s32[]{:T(128)}, f32[128,64,256]{2,1,0:T(8,128)}, s32[]{:T(128)}, bf16[8,128]{1,0:T(8,128)(2,1)S(1)}, bf16[8,128,64,256]{3,2,1,0:T(8,128)(2,1)}, /*index=5*/s32[]{:T(128)}, s32[]{:T(128)}) while((s32[]{:T(128)}, f32[128,64,256]{2,1,0:T(8,128)}, s32[]{:T(128)}, bf16[8,128]{1,0:T(8,128)(2,1)S(1)}, ...), condition=%wide.region_12.13_spmd.clone, body=%wide.region_11.12_spmd.clone.sunk | while | flops 10485892 | bytes 20972912 | solution.py:39
  786.0 6.2 fusion.172
  792.2 7.9 fusion.172
  800.1 8.0 fusion.172
  808.1 7.8 fusion.172
  815.9 7.8 fusion.172
  823.8 7.9 fusion.172
  831.7 8.0 fusion.172
  839.7 7.8 fusion.172
  847.5 8.5 fusion.66
  857.2 6.5 copy.112
  863.7 4.5 slice.125
  868.8 5.0 fusion.59
  874.5 20.1 %all-gather.3 = f32[8,1,128]{2,1,0:T(1,128)S(1)} all-gather(f32[1,1,128]{2,1,0:T(1,128)S(1)} %bitcast.414), channel_id=2, replica_groups=mesh['group'=4,'resp'=8] {'resp'}, dimensions={0}, use_global_device_ids=true | all-gather | bytes 4608 | tf_op jit(solution)/shard_map/all_gather | solution.py:49
  897.5 10.2 multiply_bitcast_fusion
  908.1 104.3 %all-reduce.23.cloned.1.call-done = bf16[4,32,64,256]{3,2,1,0:T(8,128)(2,1)} async-done(((bf16[4,32,64,256]{3,2,1,0:T(8,128)(2,1)}), bf16[4,32,64,256]{3,2,1,0:T(8,128)(2,1)}) %all-reduce.23.cloned.1.call-update) | async-done | bytes 4194320 | tf_op jit(solution)/shard_map/psum | solution.py:44
  1015.4 2.5 broadcast_in_dim.160
  1017.9 2.4 broadcast_in_dim.159
  1020.4 93.9 %while.54 = (s32[]{:T(128)}, bf16[4,256,256]{1,2,0:T(8,128)(2,1)}, bf16[4,256,256]{1,2,0:T(8,128)(2,1)}, bf16[4,256,32,64]{1,3,2,0:T(8,128)(2,1)}, f32[4,256,32]...) while((s32[]{:T(128)}, bf16[4,256,256]{1,2,0:T(8,128)(2,1)}, ...), condition=%wide.region_20.21_spmd, body=%wide.region_14.20_spmd.sunk | while | flops 1485438976 | bytes 30081284 | solution.py:126
  1028.8 6.4 fusion.166
  1037.9 4.5 fusion.170
  1052.3 6.4 fusion.166
  1061.4 4.5 fusion.170
  1075.7 6.4 fusion.166
  1084.9 4.5 fusion.170
  1099.2 6.4 fusion.166
  1108.3 4.5 fusion.170
  1117.5 6.4 fusion.65
  1123.9 39.1 %multiply_reduce_fusion.4 = (f32[10240]{0:T(1024)S(1)}, f32[10240]{0:T(1024)S(1)}, f32[10240]{0:T(1024)S(1)}, f32[10240]{0:T(1024)S(1)}, f32[10240]{0:T(1024)S(1)}) fusion(f32[259,10240]{0,1:T(8,128)} %maximum_convert_fusion, f32[256,10240]{0,1:T(8,128)} %get-tuple-element.683, bf16[256,8192]{0,1:T(8,128)(2,1)S(1)} %bitcast.363, ...), kind=kLoop, calls=%fused_computation.75 | loop fusion | flops 62863360 | bytes 57876480 | tf_op jit(solution)/shard_map/transpose(jvp())/reduce_sum | solution.py:73
  1163.0 106.7 %all-reduce.25.cloned.1.call-done = bf16[128,64,256]{2,1,0:T(8,128)(2,1)} async-done(((bf16[128,64,256]{2,1,0:T(8,128)(2,1)}), bf16[128,64,256]{2,1,0:T(8,128)(2,1)}) %all-reduce.25.cloned.1.call-update) | async-done | bytes 4194320 | tf_op jit(solution)/shard_map/psum | solution.py:211
  1269.8 2.9 convert_multiply_fusion.5
  1275.9 27.9 %multiply_reduce_fusion.8 = (f32[10240]{0:T(1024)S(1)}, f32[10240]{0:T(1024)S(1)}, f32[10240]{0:T(1024)S(1)}, f32[10240]{0:T(1024)S(1)}, f32[10240]{0:T(1024)S(1)}) fusion(f32[131,10240]{0,1:T(8,128)} %copy-done, f32[128]{0:T(128)S(1)} %copy-done.33, f32[128]{0:T(128)S(1)} %copy-done.37, f32[128]{0:T(128)S(1)} %copy-done.35, ...), kind=kLoop, calls=%fused_computation.99 | loop fusion | flops 32716800 | bytes 28780032 | tf_op jit(solution)/shard_map/transpose(jvp())/reduce_sum | solution.py:73
  1306.4 5.8 fusion.57
  1313.1 40.2 %all-reduce.18 = (f32[10240]{0:T(1024)}, f32[3,128]{1,0:T(4,128)}) all-reduce(f32[10240]{0:T(1024)S(1)} %add.312, f32[3,128]{1,0:T(4,128)S(1)} %add_add_fusion.1), channel_id=1, replica_groups=mesh['group'=4,'resp'=8] {'group','resp'}, use_global_device_ids=true, to_apply=%region_35.36 | all-reduce | flops 10624 | bytes 84992 | tf_op jit(solution)/shard_map/psum | solution.py:218
  1353.3 72.7 %all-reduce.27.cloned.1.call-done = f32[4,10240]{1,0:T(4,128)} async-done(((f32[4,10240]{1,0:T(4,128)}), f32[4,10240]{1,0:T(4,128)}) %all-reduce.27.cloned.1.call-update) | async-done | bytes 163856 | tf_op jit(solution)/shard_map/psum | solution.py:218
  (274 shorter events, 79.6 us)
Async XLA Ops:
  7.2 778.8 %all-gather.6.cloned.1.call-start = ((), (), s32[]{:S(2)}) async-start(), calls=%async_computation | async-start | bytes 37748736 | tf_op jit(solution)/shard_map/all_gather | solution.py:22
  10.4 9.2 copy-start.40
  10.5 9.8 copy-start.39
  10.5 9.9 copy-start.14
  10.5 10.5 copy-start.21
  14.7 7.2 collective-permute-start
  20.3 120.2 %copy-start.23 = (f32[128]{0:T(128)}, f32[128]{0:T(128)S(1)}, u32[]{:S(2)}) copy-start(f32[128]{0:T(128)S(1)} %get-tuple-element.701) | copy-start | bytes 1540
  20.3 120.2 %copy-start.27 = (f32[128]{0:T(128)}, f32[128]{0:T(128)S(1)}, u32[]{:S(2)}) copy-start(f32[128]{0:T(128)S(1)} %get-tuple-element.700) | copy-start | bytes 1540
  20.6 94.8 %copy-start.25 = (f32[128]{0:T(128)}, f32[128]{0:T(128)S(1)}, u32[]{:S(2)}) copy-start(f32[128]{0:T(128)S(1)} %get-tuple-element.696) | copy-start | bytes 1540
  20.8 6.5 copy-start.7
  21.7 5.6 copy-start.29
  21.7 5.6 copy-start.32
  21.8 5.6 copy-start.34
  21.8 5.6 copy-start.36
  21.9 19.8 %copy-start.18 = (f32[128,4,32]{0,2,1:T(8,128)}, f32[128,4,32]{0,2,1:T(8,128)S(1)}, u32[]{:S(2)}) copy-start(f32[128,4,32]{0,2,1:T(8,128)S(1)} %fusion.86) | copy-start | bytes 196612
  24.0 3.3 copy-start.20
  27.3 14.2 copy-start
  41.5 6.0 copy-start.1
  41.5 6.0 copy-start.10
  41.7 5.8 copy-start.3
  41.7 73.6 %copy-start.22 = (bf16[1,1,256,128]{3,2,1,0:T(8,128)(2,1)S(1)}, bf16[1,1,256,128]{3,2,1,0:T(8,128)(2,1)}, u32[]{:S(2)}) copy-start(bf16[1,1,256,128]{3,2,1,0:T(8,128)(2,1)} %param.21) | copy-start | bytes 196612
  47.6 964.9 %all-reduce.23.cloned.1.call-start = ((), (), s32[]{:S(2)}) async-start(), calls=%async_computation.1 | async-start | bytes 8388608 | tf_op jit(solution)/shard_map/psum | solution.py:44
  115.4 779.2 %copy-start.12 = (bf16[1,1,256,128]{2,3,1,0:T(8,128)(2,1)}, bf16[1,1,256,128]{2,3,1,0:T(8,128)(2,1)S(1)}, u32[]{:S(2)}) copy-start(bf16[1,1,256,128]{2,3,1,0:T(8,128)(2,1)S(1)} %copy.102) | copy-start | bytes 196612
  856.1 413.7 %all-reduce.25.cloned.1.call-start = ((), (), s32[]{:S(2)}) async-start(), calls=%async_computation.2 | async-start | bytes 8388608 | tf_op jit(solution)/shard_map/psum | solution.py:211
  1021.9 6.9 copy-start.16
  1021.9 6.9 copy-start.9
  1045.4 6.9 copy-start.16
  1045.4 6.8 copy-start.9
  1068.9 6.9 copy-start.16
  1068.9 6.9 copy-start.9
  1092.3 6.9 copy-start.16
  1092.4 6.9 copy-start.9
  1114.3 2.9 copy-start.13
  1114.3 2.9 copy-start.17
  1114.3 2.9 copy-start.24
  1114.3 2.9 copy-start.28
  1114.3 3.2 copy-start.31
  1114.3 311.6 %all-reduce.27.cloned.1.call-start = ((), (), s32[]{:S(2)}) async-start(), calls=%async_computation.3 | async-start | bytes 327680 | tf_op jit(solution)/shard_map/psum | solution.py:218
  1117.5 6.4 copy-start.5
  1117.5 6.4 copy-start.6
  1163.0 109.7 %copy-start.4 = (bf16[128,8192]{0,1:T(8,128)(2,1)S(1)}, bf16[128,8192]{0,1:T(8,128)(2,1)}, u32[]{:S(2)}) copy-start(bf16[128,8192]{0,1:T(8,128)(2,1)} %copy-done.3) | copy-start | bytes 6291460
  1163.0 109.7 %copy-start.19 = (f32[128,4,32]{0,2,1:T(8,128)S(1)}, f32[128,4,32]{0,2,1:T(8,128)}, u32[]{:S(2)}) copy-start(f32[128,4,32]{0,2,1:T(8,128)} %copy-done.18) | copy-start | bytes 196612
  1272.7 1.8 copy-start.2
  1275.9 29.1 %copy-start.8 = (f32[128,128]{1,0:T(8,128)S(1)}, f32[128,128]{1,0:T(8,128)}, u32[]{:S(2)}) copy-start(f32[128,128]{1,0:T(8,128)} %copy-done.7) | copy-start | bytes 196612
  1275.9 29.1 %copy-start.15 = (bf16[1,128,128]{2,1,0:T(8,128)(2,1)S(1)}, bf16[1,128,128]{2,1,0:T(8,128)(2,1)}, u32[]{:S(2)}) copy-start(bf16[1,128,128]{2,1,0:T(8,128)(2,1)} %param.18) | copy-start | bytes 98308
  1275.9 29.1 %copy-start.26 = (f32[128]{0:T(128)S(1)}, f32[128]{0:T(128)}, u32[]{:S(2)}) copy-start(f32[128]{0:T(128)} %copy-done.25) | copy-start | bytes 1540
  1275.9 29.1 %copy-start.30 = (f32[128]{0:T(128)S(1)}, f32[128]{0:T(128)}, u32[]{:S(2)}) copy-start(f32[128]{0:T(128)} %copy-done.29) | copy-start | bytes 1540
  1306.4 6.7 copy-start.38
  (4 other events, 5.8 us)
Sparse Core Ops, SparseCore 0:
  47.7 738.2 all-gather.5
  856.2 156.1 all-reduce.22
  1114.4 155.2 all-reduce.24
  1305.0 120.9 all-reduce.26
where the time goes:
time: 1450 us; the launch traced here: 1430 us
  waiting for transfers between devices  635 us (44%)
  blocking collectives  395 us (27%)
  other arithmetic  238 us (16%)
  local copies, waits for them, and re-layouts  76.5 us (5%)
  matrix products  64.5 us (4%)
  between operations  18.1 us (1%)
    all_gather x1, waiting for transfers between devices, prefix(): lax.all_gather(part.astype(kind), axis)  351 us
    psum x1, blocking collectives, from_root(): return lax.psum(block, axis)  246 us
    psum x1, waiting for transfers between devices, shards(): grad_state = lax.psum(begin_grad, 'resp').astype(jnp.float32)  107 us
    psum x1, waiting for transfers between devices, from_root(): return lax.psum(block, axis)  104 us
    psum x1, waiting for transfers between devices, shards(): lax.psum((resp_grads[0] + prompt_grads[0], resp_grads[1] + prompt_grads[1...  72.7 us
    reduce_sum x2, other arithmetic, conv_silu(): conv_w[taps_back - offset][None, :]  67 us
    psum x1, blocking collectives, shards(): total_reward = lax.psum(reward[0, 0], 'resp')  63.7 us
    select_n x8, other arithmetic, prefix_lap(): return jax.tree.map(lambda a, b: jnp.where(reached, a, b), new, before)  61.5 us
  transfers between devices with their start and end apart: 5, of which 4 were waited for; matrix products, arithmetic and copies ran while one was open for 10% of the time, Pallas kernels for 0%

commit v1 on v0

v1 whole, which is shorter than its diff:
```python
import functools

import jax
import jax.numpy as jnp
from jax import lax
from jax.experimental import pallas as pl
from jax.experimental.pallas import tpu as pltpu
from jax.sharding import PartitionSpec as P

H = 128
PS = 64
N = 256
G = 4
K = 4
HG = H // G
XC = H * PS
GX = HG * PS
LANES = 128
PAD = 8
VMEM_LIMIT = 50 * 2**20

f32 = jnp.float32
bf16 = jnp.bfloat16

NN = (((1,), (0,)), ((), ()))
NT = (((1,), (1,)), ((), ()))


def dot(a, b, dims=NN, precision=None):
    return lax.dot_general(a, b, dims, precision=precision, preferred_element_type=f32)


def halves(v):
    hi = v.astype(bf16)
    return hi, (v - hi.astype(f32)).astype(bf16)


def indicator(first, width):
    row = lax.broadcasted_iota(jnp.int32, (LANES, width), 0)
    head = lax.shift_right_logical(lax.broadcasted_iota(jnp.int32, (LANES, width), 1), 6)
    return jnp.where(row - first == head, 1.0, 0.0).astype(bf16)


def expand(v, ind):
    hi, lo = halves(v)
    return dot(hi, ind) + dot(lo, ind)


def head_sums(z_hi, z_lo, ind):
    return dot(z_hi, ind, NT) + dot(z_lo, ind, NT)


def triangle(n, keep):
    i = lax.broadcasted_iota(jnp.int32, (n, n), 0)
    j = lax.broadcasted_iota(jnp.int32, (n, n), 1)
    return jnp.where(keep(i, j), 1.0, 0.0).astype(f32)


def tri_sum(tri, v):
    return dot(tri, v, precision=lax.Precision.HIGHEST)


def softplus(z):
    return jnp.maximum(z, 0.0) + jnp.log1p(jnp.exp(-jnp.abs(z)))


def sigmoid(z):
    return 0.5 * jnp.tanh(0.5 * z) + 0.5


def taps_of(ext, lanes, row, rows):
    return [ext[pl.ds(PAD - K + 1 + k + row, rows), lanes] for k in range(K)]


def conv_pre(taps, wb, masks=None):
    total = wb[K : K + 1] + wb[K - 1 : K] * taps[K - 1]
    for k in range(K - 1):
        term = wb[k : k + 1] * taps[k]
        if masks is not None:
            term = term * masks[k]
        total = total + term
    return total


def act_and_slope(pre):
    sig = sigmoid(pre)
    act = pre * sig
    return act, sig + act * (1.0 - sig)


def fold8(v):
    return jnp.sum(v.reshape(v.shape[0] // 8, 8, v.shape[1]), axis=0)


def lane_loop(width, body, step=LANES):
    def one(i, _):
        body(pl.ds(pl.multiple_of(i * step, step), step))
        return 0

    lax.fori_loop(0, width // step, one, 0)


RC = 64


def conv_forward(u, tail, wb, ext, act, slope, rows, width):
    def body(lanes):
        ext[0:PAD, lanes] = tail[:, lanes]
        ext[PAD : PAD + rows, lanes] = u[:, lanes].astype(f32)
        w = wb[:, lanes]
        for r in range(0, rows, RC):
            a, s = act_and_slope(conv_pre(taps_of(ext, lanes, r, RC), w))
            act[r : r + RC, lanes] = a.astype(bf16)
            if slope is not None:
                slope[r : r + RC, lanes] = s

    lane_loop(width, body)


def conv_backward(ext, slope, lanes, cotangent, grad, rows):
    sums = [jnp.zeros((8, LANES), f32) for _ in range(K + 1)]
    for r in range(0, rows, RC):
        d = cotangent(r) * slope[r : r + RC, lanes]
        taps = taps_of(ext, lanes, r, RC)
        for k in range(K):
            sums[k] = sums[k] + fold8(d * taps[k])
        sums[K] = sums[K] + fold8(d)
    for k in range(K + 1):
        grad[k : k + 1, lanes] = jnp.sum(sums[k], axis=0, keepdims=True)


def steps_kernel(len_ref, dt, hp, step, cum, cum_t, decay_in):
    rows = dt.shape[0]
    s = softplus(dt[...].astype(f32) + hp[1:2])
    logd = -jnp.exp(hp[0:1]) * s
    c = tri_sum(triangle(rows, lambda i, j: i >= j), logd)
    step[...] = s
    cum[...] = c
    cum_t[...] = c.T
    t = lax.broadcasted_iota(jnp.int32, c.shape, 0)
    decay_in[...] = jnp.where(t < len_ref[0, 0], jnp.exp(c), 0.0)


def resp_state_kernel(per, adv, u_c, tail_c, wb_c, dy, decay_in, state, weighted, c_out, ext, c_t):
    slab = pl.program_id(0)
    rows, width = dy.shape

    @pl.when(slab % per == 0)
    def _():
        conv_forward(u_c, tail_c, wb_c, ext, c_out, None, rows, N)
        c_t[...] = c_out[...].astype(f32).T.astype(bf16)

    ind = indicator(slab * (width // PS), width)
    a = (dy[...].astype(f32) * expand(decay_in[...], ind)).astype(bf16)
    weighted[...] = a
    state[0] = (dot(c_t[...], a) * adv[0, 0]).astype(bf16)


def resp_mid_kernel(
    len_ref, u_x, u_b, tail_x, tail_b, wb_x, wb_b, c_act, dy, step, cum, cum4, cum_t4, skip,
    grad_x, grad_b, dc, row_out, col_out,
    ext, ext_b, x_s, xs_s, b_s, dym, slope, slope_b, step_e, y_s, t_s,
    a1, bm, sw_e, u_off, y_off, z_hi, z_lo,
):
    g = pl.program_id(0)
    rows = u_x.shape[0]
    half = rows // 2
    conv_forward(u_x, tail_x, wb_x, ext, x_s, slope, rows, GX)
    conv_forward(u_b, tail_b, wb_b, ext_b, b_s, slope_b, rows, N)
    ind = indicator(g * HG, GX)
    step_e[...] = expand(step[...], ind)
    cum_v = cum[...]
    mid = cum_v[half - 1 : half]
    sw_e[...] = expand(jnp.exp(mid - cum_v[:half]) * step[:half], ind)
    y_off[...] = expand(jnp.exp(cum_v[half:] - mid), ind)
    live = jnp.where(lax.broadcasted_iota(jnp.int32, (rows, LANES), 0) < len_ref[0, 0], 1.0, 0.0)

    def prepare(lanes):
        d = dy[:, lanes].astype(f32) * live
        dym[:, lanes] = d.astype(bf16)
        x = x_s[:, lanes].astype(f32)
        xs_s[:, lanes] = (x * step_e[:, lanes]).astype(bf16)
        bm[:, lanes] = (x[:half] * sw_e[:, lanes]).astype(bf16)
        a1[:, lanes] = (d[half:] * y_off[:, lanes]).astype(bf16)

    lane_loop(GX, prepare)

    c_v, b_v = c_act[...], b_s[...]
    c0, c1, b0, b1 = c_v[:half], c_v[half:], b_v[:half], b_v[half:]
    i = lax.broadcasted_iota(jnp.int32, (half, half), 0)
    j = lax.broadcasted_iota(jnp.int32, (half, half), 1)
    lane = lax.broadcasted_iota(jnp.int32, (half, LANES), 1)
    first = jnp.where(lane < PS, 1.0, 0.0).astype(bf16)
    second = jnp.where(lane >= PS, 1.0, 0.0).astype(bf16)

    y_off[...] = dot(dot(c1, b0, NT).astype(bf16), bm[...])
    u_off[...] = dot(dot(b0, c1, NT).astype(bf16), a1[...])
    d10 = dot(a1[...], bm[...], NT)

    d_diag = []
    for q, (c_q, b_q) in enumerate(((c0, b0), (c1, b1))):
        r = slice(q * half, (q + 1) * half)
        lower = jnp.where(i >= j, dot(c_q, b_q, NT), 0.0)
        upper = jnp.where(j >= i, dot(b_q, c_q, NT), 0.0)
        d_sc = jnp.zeros((half, half), f32)
        for p in range(HG // 2):
            lanes = slice(p * LANES, (p + 1) * LANES)
            xs_p, dy_p = xs_s[r, lanes], dym[r, lanes]
            xb = jnp.concatenate([xs_p * first, xs_p * second], axis=0)
            dyb = jnp.concatenate([dy_p * first, dy_p * second], axis=0)
            d_m = dot(dy_p, xb, NT)
            mats, mats_t = [], []
            for a in range(2):
                h = 2 * p + a
                gap = jnp.exp(-jnp.abs(cum4[0, r, h : h + 1] - cum_t4[0, h : h + 1, r]))
                d_sc = d_sc + d_m[:, a * half : (a + 1) * half] * gap
                mats.append((gap * lower).astype(bf16))
                mats_t.append((gap * upper).astype(bf16))
            y_s[r, lanes] = dot(jnp.concatenate(mats, axis=1), xb)
            t_s[r, lanes] = dot(jnp.concatenate(mats_t, axis=1), dyb)
        d_diag.append(jnp.where(i >= j, d_sc, 0.0))

    d00, d11 = d_diag
    dc[:half] = dot(d00.astype(bf16), b0)
    dc[half:] = dot(d11.astype(bf16), b1) + dot(d10.astype(bf16), b0)
    db0 = dot(d00.T.astype(bf16), c0) + dot(d10.T.astype(bf16), c1)
    db1 = dot(d11.T.astype(bf16), c1)
    db = jnp.concatenate([db0, db1], axis=0)
    for k in range(N // LANES):
        lanes = slice(k * LANES, (k + 1) * LANES)
        conv_backward(ext_b, slope_b, lanes, lambda r: db[r : r + RC, lanes], grad_b, rows)

    def put(z, r, lanes):
        hi, lo = halves(z)
        z_hi[r : r + RC, lanes] = hi
        z_lo[r : r + RC, lanes] = lo

    def row_products(lanes):
        for r in range(0, rows, RC):
            z = dym[r : r + RC, lanes].astype(f32) * y_s[r : r + RC, lanes]
            if r >= half:
                o = r - half
                z = z + a1[o : o + RC, lanes].astype(f32) * y_off[o : o + RC, lanes]
            put(z, r, lanes)

    lane_loop(GX, row_products)
    row_sum = head_sums(z_hi[...], z_lo[...], ind)

    def finish(lanes):
        d_skip = jnp.zeros((8, LANES), f32)
        for r in range(0, rows, RC):
            t = t_s[r : r + RC, lanes]
            z = xs_s[r : r + RC, lanes].astype(f32) * t
            if r < half:
                z = z + bm[r : r + RC, lanes].astype(f32) * u_off[r : r + RC, lanes]
            put(z, r, lanes)
            d_skip = d_skip + fold8(
                dym[r : r + RC, lanes].astype(f32) * x_s[r : r + RC, lanes].astype(f32)
            )

        def cotangent(r):
            d = step_e[r : r + RC, lanes] * t_s[r : r + RC, lanes]
            d = d + skip[:, lanes] * dym[r : r + RC, lanes].astype(f32)
            if r < half:
                d = d + sw_e[r : r + RC, lanes] * u_off[r : r + RC, lanes]
            return d

        conv_backward(ext, slope, lanes, cotangent, grad_x, rows)
        grad_x[K + 1 : K + 2, lanes] = jnp.sum(d_skip, axis=0, keepdims=True)

    lane_loop(GX, finish)
    col_sum = head_sums(z_hi[...], z_lo[...], ind)

    @pl.when(g == 0)
    def _():
        row_out[...] = row_sum
        col_out[...] = col_sum

    @pl.when(g > 0)
    def _():
        row_out[...] += row_sum
        col_out[...] += col_sum


def resp_end_kernel(
    u_c, tail_c, wb_c, c_act, weighted, start, dc, row_in, col_in, step, dt, hp,
    grad_c, grad_h, ext, c_s, slope, total,
):
    g = pl.program_id(0)
    rows = u_c.shape[0]
    per, _, width = start.shape
    conv_forward(u_c, tail_c, wb_c, ext, c_s, slope, rows, N)
    d = dc[...]

    @pl.when(g == 0)
    def _():
        total[...] = row_in[...] - col_in[...]

    for s in range(per):
        a = weighted[:, s * width : (s + 1) * width]
        st = start[s]
        z_hi, z_lo = halves(a.astype(f32) * dot(c_act[...], st))
        total[...] += head_sums(z_hi, z_lo, indicator(g * HG + s * (width // PS), width))
        d = d + dot(a, st, NT)
    for k in range(N // LANES):
        lanes = slice(k * LANES, (k + 1) * LANES)
        conv_backward(ext, slope, lanes, lambda r: d[r : r + RC, lanes], grad_c, rows)

    @pl.when(g == pl.num_programs(0) - 1)
    def _():
        d_log = tri_sum(triangle(rows, lambda i, j: j >= i), total[...])
        rate = -jnp.exp(hp[0:1])
        s = step[...]
        d_step = col_in[...] / s + rate * d_log
        grad_h[...] = jnp.zeros_like(grad_h)
        grad_h[0:1] = jnp.sum(d_log * rate * s, axis=0, keepdims=True)
        grad_h[1:2] = jnp.sum(
            d_step * sigmoid(dt[...].astype(f32) + hp[1:2]), axis=0, keepdims=True
        )


RB = 256


def prompt_conv(v, masks, wb, ext, act, slope, row, width):
    def body(lanes):
        ext[PAD : PAD + RB, lanes] = v[pl.ds(row, RB), lanes].astype(f32)
        w = wb[:, lanes]
        for r in range(0, RB, RC):
            m = [masks[pl.ds(row + r, RC), k : k + 1] for k in range(K - 1)]
            a, s = act_and_slope(conv_pre(taps_of(ext, lanes, r, RC), w, m))
            act[r : r + RC, lanes] = a.astype(bf16)
            if slope is not None:
                slope[r : r + RC, lanes] = s

    lane_loop(width, body)


def prompt_state_kernel(v, masks, wb, hp, start, weight, step, ext, act, acc):
    rows = v.shape[0]
    width = start.shape[1]
    ind = indicator(0, width)
    later = triangle(RB, lambda i, j: j > i)
    ahead = jnp.zeros((1, LANES), f32)
    acc[...] = jnp.zeros_like(acc)
    for row in range(rows - RB, -1, -RB):
        s = softplus(v[row : row + RB, width + N :].astype(f32) + hp[1:2])
        logd = -jnp.exp(hp[0:1]) * s
        after = tri_sum(later, logd) + ahead
        ahead = ahead + jnp.sum(logd, axis=0, keepdims=True)
        w = masks[row : row + RB, K - 1 : K] * jnp.exp(after) * s
        step[row : row + RB] = s
        weight[row : row + RB] = w
        if row:
            ext[0:PAD] = v[row - 16 : row, : width + N].astype(f32)[16 - PAD :]
        else:
            ext[0:PAD] = jnp.zeros((PAD, width + N), f32)
        prompt_conv(v, masks, wb, ext, act, None, row, width + N)
        wx = (act[:, :width].astype(f32) * expand(w, ind)).astype(bf16)
        acc[...] += dot(act[:, width:].astype(f32).T.astype(bf16), wx)
    start[...] = acc[...].astype(bf16)


def prompt_grad_kernel(
    v, masks, wb, hp, weight, step, states,
    grad, grad_h, ext, act, slope, g_s, d_s, sums,
):
    rows = v.shape[0]
    width = states.shape[2]
    ind = indicator(0, width)
    earlier = triangle(RB, lambda i, j: j < i)
    total = states[0].astype(f32)
    for k in range(1, states.shape[0]):
        total = total + states[k].astype(f32)
    g_s[...] = total.astype(bf16)
    behind = jnp.zeros((1, LANES), f32)
    rate = -jnp.exp(hp[0:1])
    d_rate = jnp.zeros((1, LANES), f32)
    d_bias = jnp.zeros((1, LANES), f32)
    sums[...] = jnp.zeros_like(sums)
    for row in range(0, rows, RB):
        if row:
            ext[0:PAD] = v[row - 16 : row, : width + N].astype(f32)[16 - PAD :]
        else:
            ext[0:PAD] = jnp.zeros((PAD, width + N), f32)
        prompt_conv(v, masks, wb, ext, act, slope, row, width + N)
        w_e = expand(weight[row : row + RB], ind)
        t = dot(act[:, width:], g_s[...])
        wx = (act[:, :width].astype(f32) * w_e).astype(bf16)
        d_s[:, :width] = t * w_e
        d_s[:, width:] = dot(wx, g_s[...], NT)
        z_hi, z_lo = halves(wx.astype(f32) * t)
        q = head_sums(z_hi, z_lo, ind)
        d_log = tri_sum(earlier, q) + behind
        behind = behind + jnp.sum(q, axis=0, keepdims=True)
        s = step[row : row + RB]
        d_step = q / s + rate * d_log
        z = v[row : row + RB, width + N :].astype(f32) + hp[1:2]
        d_rate = d_rate + jnp.sum(d_log * rate * s, axis=0, keepdims=True)
        d_bias = d_bias + jnp.sum(d_step * sigmoid(z), axis=0, keepdims=True)

        def back(lanes):
            acc = [jnp.zeros((8, LANES), f32) for _ in range(K + 1)]
            for r in range(0, RB, RC):
                d = d_s[r : r + RC, lanes] * slope[r : r + RC, lanes]
                taps = taps_of(ext, lanes, r, RC)
                for k in range(K):
                    part = d * taps[k]
                    if k < K - 1:
                        part = part * masks[pl.ds(row + r, RC), k : k + 1]
                    acc[k] = acc[k] + fold8(part)
                acc[K] = acc[K] + fold8(d)
            for k in range(K + 1):
                sums[k : k + 1, lanes] += jnp.sum(acc[k], axis=0, keepdims=True)

        lane_loop(width + N, back)
    grad[...] = sums[...]
    grad_h[...] = jnp.zeros_like(grad_h)
    grad_h[0:1] = d_rate
    grad_h[1:2] = d_bias


def params(*semantics):
    return pltpu.CompilerParams(vmem_limit_bytes=VMEM_LIMIT, dimension_semantics=semantics or None)


SMEM = pl.BlockSpec(memory_space=pltpu.SMEM)


def whole(shape):
    return pl.BlockSpec(shape, lambda *_: (0,) * len(shape))


def sds(shape, dtype):
    return jax.ShapeDtypeStruct(shape, dtype)


def response_steps(length, dt, hp):
    rows = dt.shape[0]
    square = sds((rows, H), f32)
    return pl.pallas_call(
        steps_kernel,
        out_shape=(square, square, sds((H, rows), f32), square),
        in_specs=[SMEM, pl.BlockSpec(), pl.BlockSpec()],
        compiler_params=params(),
        name="resp_steps",
    )(length, dt, hp)


def response_state(n, scale, u, tail, wb, dy, decay_in):
    rows = u.shape[0]
    per = n // G
    width = XC // n
    c_at = lambda i: (0, XC // N + G + i // per)
    return pl.pallas_call(
        functools.partial(resp_state_kernel, per),
        grid=(n,),
        in_specs=[
            SMEM,
            pl.BlockSpec((rows, N), c_at),
            pl.BlockSpec((PAD, N), c_at),
            pl.BlockSpec((PAD, N), c_at),
            pl.BlockSpec((rows, width), lambda i: (0, i)),
            whole((rows, H)),
        ],
        out_specs=[
            pl.BlockSpec((1, N, width), lambda i: (i, 0, 0)),
            pl.BlockSpec((rows, width), lambda i: (0, i)),
            pl.BlockSpec((rows, N), lambda i: (0, i // per)),
        ],
        out_shape=(sds((n, N, width), bf16), sds((rows, XC), bf16), sds((rows, G * N), bf16)),
        scratch_shapes=[pltpu.VMEM((PAD + rows, N), f32), pltpu.VMEM((N, rows), bf16)],
        compiler_params=params("arbitrary"),
        cost_estimate=pl.CostEstimate(
            flops=2 * rows * N * XC, bytes_accessed=14 * 2**20, transcendentals=rows * G * N
        ),
        name="resp_state",
    )(scale, u, tail, wb, dy, decay_in)


def response_mid(length, u, tail, wb, c_act, dy, step, cum, cum4, cum_t4, skip):
    rows = u.shape[0]
    half = rows // 2
    x_at = lambda g: (0, g)
    b_at = lambda g: (0, XC // N + g)
    v = pltpu.VMEM
    return pl.pallas_call(
        resp_mid_kernel,
        grid=(G,),
        in_specs=[
            SMEM,
            pl.BlockSpec((rows, GX), x_at),
            pl.BlockSpec((rows, N), b_at),
            pl.BlockSpec((PAD, GX), x_at),
            pl.BlockSpec((PAD, N), b_at),
            pl.BlockSpec((PAD, GX), x_at),
            pl.BlockSpec((PAD, N), b_at),
            pl.BlockSpec((rows, N), x_at),
            pl.BlockSpec((rows, GX), x_at),
            whole((rows, H)),
            whole((rows, H)),
            pl.BlockSpec((1, rows, HG), lambda g: (g, 0, 0)),
            pl.BlockSpec((1, HG, rows), lambda g: (g, 0, 0)),
            pl.BlockSpec((1, GX), x_at),
        ],
        out_specs=[
            pl.BlockSpec((PAD, GX), x_at),
            pl.BlockSpec((PAD, N), x_at),
            pl.BlockSpec((rows, N), x_at),
            whole((rows, H)),
            whole((rows, H)),
        ],
        out_shape=(
            sds((PAD, XC), f32),
            sds((PAD, G * N), f32),
            sds((rows, G * N), f32),
            sds((rows, H), f32),
            sds((rows, H), f32),
        ),
        scratch_shapes=[
            v((PAD + rows, GX), f32),
            v((PAD + rows, N), f32),
            v((rows, GX), bf16),
            v((rows, GX), bf16),
            v((rows, N), bf16),
            v((rows, GX), bf16),
            v((rows, GX), f32),
            v((rows, N), f32),
            v((rows, GX), f32),
            v((rows, GX), f32),
            v((rows, GX), f32),
            v((half, GX), bf16),
            v((half, GX), bf16),
            v((half, GX), f32),
            v((half, GX), f32),
            v((half, GX), f32),
            v((rows, GX), bf16),
            v((rows, GX), bf16),
        ],
        compiler_params=params("arbitrary"),
        cost_estimate=pl.CostEstimate(
            flops=12 * 2**30, bytes_accessed=12 * 2**20, transcendentals=rows * half * H
        ),
        name="resp_mid",
    )(length, u, u, tail, tail, wb, wb, c_act, dy, step, cum, cum4, cum_t4, skip)


def response_end(u, tail, wb, c_act, weighted, start, dc, row_in, col_in, step, dt, hp):
    rows = u.shape[0]
    n, _, width = start.shape
    per = n // G
    c_at = lambda g: (0, XC // N + G + g)
    g_at = lambda g: (0, g)
    v = pltpu.VMEM
    return pl.pallas_call(
        resp_end_kernel,
        grid=(G,),
        in_specs=[
            pl.BlockSpec((rows, N), c_at),
            pl.BlockSpec((PAD, N), c_at),
            pl.BlockSpec((PAD, N), c_at),
            pl.BlockSpec((rows, N), g_at),
            pl.BlockSpec((rows, GX), g_at),
            pl.BlockSpec((per, N, width), lambda g: (g, 0, 0)),
            pl.BlockSpec((rows, N), g_at),
            whole((rows, H)),
            whole((rows, H)),
            whole((rows, H)),
            whole((rows, H)),
            whole((PAD, H)),
        ],
        out_specs=[pl.BlockSpec((PAD, N), g_at), whole((PAD, H))],
        out_shape=(sds((PAD, G * N), f32), sds((PAD, H), f32)),
        scratch_shapes=[
            v((PAD + rows, N), f32),
            v((rows, N), bf16),
            v((rows, N), f32),
            v((rows, H), f32),
        ],
        compiler_params=params("arbitrary"),
        cost_estimate=pl.CostEstimate(
            flops=4 * rows * N * XC, bytes_accessed=12 * 2**20, transcendentals=rows * G * N
        ),
        name="resp_end",
    )(u, tail, wb, c_act, weighted, start, dc, row_in, col_in, step, dt, hp)


def prompt_state(v, masks, wb, hp, width):
    rows = v.shape[0]
    s = pltpu.VMEM
    return pl.pallas_call(
        prompt_state_kernel,
        out_shape=(sds((N, width), bf16), sds((rows, LANES), f32), sds((rows, LANES), f32)),
        scratch_shapes=[
            s((PAD + RB, width + N), f32),
            s((RB, width + N), bf16),
            s((N, width), f32),
        ],
        compiler_params=params(),
        cost_estimate=pl.CostEstimate(
            flops=2 * rows * N * width, bytes_accessed=4 * 2**20, transcendentals=rows * width
        ),
        name="prompt_state",
    )(v, masks, wb, hp)


def prompt_grad(v, masks, wb, hp, weight, step, states):
    rows = v.shape[0]
    width = states.shape[2]
    s = pltpu.VMEM
    return pl.pallas_call(
        prompt_grad_kernel,
        out_shape=(sds((PAD, width + N), f32), sds((PAD, LANES), f32)),
        scratch_shapes=[
            s((PAD + RB, width + N), f32),
            s((RB, width + N), bf16),
            s((RB, width + N), f32),
            s((N, width), bf16),
            s((RB, width + N), f32),
            s((PAD, width + N), f32),
        ],
        compiler_params=params(),
        cost_estimate=pl.CostEstimate(
            flops=4 * rows * N * width, bytes_accessed=8 * 2**20, transcendentals=rows * width
        ),
        name="prompt_grad",
    )(v, masks, wb, hp, weight, step, states)


def doc_number(starts, positions):
    return jnp.sum((starts[None, :] <= positions[:, None]).astype(jnp.int32), axis=1)


def prompt_masks(starts, rows):
    positions = jnp.arange(rows, dtype=jnp.int32)
    docs = doc_number(starts, positions)
    same = [doc_number(starts, positions - (K - 1 - k)) == docs for k in range(K - 1)]
    columns = jnp.stack(same + [docs == docs[rows - 1]], axis=1).astype(f32)
    return jnp.pad(columns, ((0, 0), (0, PAD - K)))


def pad_rows(a):
    return jnp.pad(a, ((0, PAD - a.shape[0]), (0, 0)))


def shards(
    prompt_in, prompt_dt, doc_starts, resp_in, resp_dt, resp_len, upstream, reward,
    conv_w, conv_b, head_params,
):
    n = lax.axis_size("resp")
    me = lax.axis_index("resp")
    hs = H // n
    width = XC // n
    per = n // G
    block = prompt_in.shape[1]
    slots = resp_in.shape[2]
    rows_in, dt_in = prompt_in[0], prompt_dt[0]
    u, dt, dy = resp_in[0, 0], resp_dt[0, 0], upstream[0, 0]

    r = reward[0, 0]
    r_hi = r.astype(bf16)
    r_mid = (r - r_hi.astype(f32)).astype(bf16)
    r_lo = (r - r_hi.astype(f32) - r_mid.astype(f32)).astype(bf16)
    tail_size = (K - 1) * rows_in.shape[1] // LANES
    small = jnp.concatenate(
        [
            rows_in[block - K + 1 :].reshape(tail_size, LANES),
            jnp.broadcast_to(jnp.stack([r_hi, r_mid, r_lo, jnp.zeros_like(r_lo)])[:, None], (4, LANES)),
            jnp.zeros((12, LANES), bf16),
        ]
    )
    small = lax.all_gather(small, "resp")
    tail_rows = small[n - 1, :tail_size].reshape(K - 1, -1).astype(f32)
    tail = jnp.pad(tail_rows, ((PAD - K + 1, 0), (0, 0)))
    rewards = jnp.sum(small[:, tail_size : tail_size + 3, 0].astype(f32), axis=1)
    scale = (r - jnp.sum(rewards) / n) / slots
    wb = pad_rows(jnp.concatenate([conv_w, conv_b[None]], axis=0))
    hp = pad_rows(head_params)

    x_parts = rows_in[:, :XC].reshape(block, n, width).transpose(1, 0, 2)
    b_parts = jnp.repeat(
        rows_in[:, XC : XC + G * N].reshape(block, G, N).transpose(1, 0, 2), per, axis=0
    )
    dt_parts = jnp.pad(
        dt_in.reshape(block, n, hs).transpose(1, 0, 2), ((0, 0), (0, 0), (0, LANES - hs))
    )
    v = lax.all_to_all(
        jnp.concatenate([x_parts, b_parts, dt_parts], axis=2), "resp", 0, 0
    ).reshape(n * block, width + N + LANES)
    masks = prompt_masks(doc_starts[0], n * block)
    my_group = me // per
    wb_mine = jnp.concatenate(
        [
            lax.dynamic_slice(wb, (0, me * width), (PAD, width)),
            lax.dynamic_slice(wb, (0, XC + my_group * N), (PAD, N)),
        ],
        axis=1,
    )
    hp_mine = jnp.pad(lax.dynamic_slice(hp, (0, me * hs), (PAD, hs)), ((0, 0), (0, LANES - hs)))

    length = resp_len.astype(jnp.int32)
    step, cum, cum_t, decay_in = response_steps(length, dt, hp)
    d_states, weighted, c_act = response_state(
        n, scale.reshape(1, 1), u, tail, wb, dy, decay_in
    )
    start_mine, weight, p_step = prompt_state(v, masks, wb_mine, hp_mine, width)
    start = lax.all_gather(start_mine, "resp")
    d_states = lax.all_to_all(d_states, "resp", 0, 0)

    cum4 = cum.reshape(slots, G, HG).transpose(1, 0, 2)
    skip = jnp.repeat(head_params[2], PS)[None, :]
    grad_x, grad_b, dc, row_in, col_in = response_mid(
        length, u, tail, wb, c_act, dy, step, cum, cum4, cum_t.reshape(G, HG, slots), skip
    )
    p_grad, p_heads = prompt_grad(v, masks, wb_mine, hp_mine, weight, p_step, d_states)
    grad_c, r_heads = response_end(
        u, tail, wb, c_act, weighted, start, dc, row_in, col_in, step, dt, hp
    )

    conv = jnp.concatenate([grad_x, grad_b, grad_c], axis=1)[: K + 1] * scale
    mine = lax.dynamic_slice(conv, (0, me * width), (K + 1, width)) + p_grad[: K + 1, :width]
    conv = lax.dynamic_update_slice(conv, mine, (0, me * width))
    at_b = XC + my_group * N
    mine = lax.dynamic_slice(conv, (0, at_b), (K + 1, N)) + p_grad[: K + 1, width:]
    conv = lax.dynamic_update_slice(conv, mine, (0, at_b))
    d_skip = jnp.sum(grad_x[K + 1].reshape(H, PS), axis=1)
    heads = jnp.concatenate([r_heads[:2], d_skip[None]], axis=0) * scale
    mine = lax.dynamic_slice(heads, (0, me * hs), (2, hs)) + p_heads[:2, :hs]
    heads = lax.dynamic_update_slice(heads, mine, (0, me * hs))
    conv, heads = lax.psum((conv, heads), ("group", "resp"))
    return conv[:K], conv[K], heads


def solution(mesh):
    in_specs = (
        P("group", "resp", None),
        P("group", "resp", None),
        P("group", None),
        P("group", "resp", None, None),
        P("group", "resp", None, None),
        P("group", "resp"),
        P("group", "resp", None, None),
        P("group", "resp"),
        P(),
        P(),
        P(),
    )
    out_specs = (P(), P(), P())
    return jax.shard_map(shards, mesh=mesh, in_specs=in_specs, out_specs=out_specs, check_vma=False)
```

time: 1450 us -> 442 us (0.30)
  waiting for transfers between devices: 635 us -> 133 us
  blocking collectives: 395 us -> 119 us
  other arithmetic: 238 us -> 5.85 us
  Pallas kernels: 0 us -> 130 us
  matrix products: 64.5 us -> 0 us
  local copies, waits for them, and re-layouts: 76.5 us -> 23 us
    all_gather x1, waiting for transfers between devices: 351 us -> 0.01 us  [shards(): start = lax.all_gather(start_mine, 'resp')]
    psum x3 -> x1, blocking collectives: 350 us -> 37.1 us  [shards(): conv, heads = lax.psum((conv, heads), ('group', 'resp'))]
    psum x3 -> x1, waiting for transfers between devices: 284 us -> 85.1 us  [shards(): conv, heads = lax.psum((conv, heads), ('group', 'resp'))]
    pallas_call x0 -> x6, Pallas kernels: none -> 130 us  [the longest x1 65.7 us: response_mid(): pl.pallas_call(resp_mid_kernel, grid=(G,), in_specs=[SMEM, pl.BlockSpec((...]
    reduce_sum x9 -> x2, other arithmetic: 79.1 us -> 2.07 us  [the longest x1 1.46 us: shards(): d_skip = jnp.sum(grad_x[K + 1].reshape(H, PS), axis=1)]
    select_n x18 -> x0, other arithmetic: 72 us -> none  [the longest x8 61.5 us: prefix_lap(): return jax.tree.map(lambda a, b: jnp.where(reached, a, b), new, before)]
    dot_general x35 -> x0, matrix products: 64.5 us -> none  [the longest x8 43.5 us: group_mix(): jnp.einsum('jts,sjp->tjp', weights_mix, x_part, preferred_element_type=jn...]
    convert_element_type x13 -> x0, other arithmetic: 55.3 us -> none  [the longest x2 42.1 us: conv_silu(): return jax.nn.silu(total).astype(jnp.bfloat16)]
  transfers between devices with their start and end apart: 5 -> 4, of which waited for: 4 -> 2; matrix products, arithmetic and copies ran while one was open for 10% -> 2% of each run, Pallas kernels for 0% -> 28%
where the time goes in v1:
time: 442 us; the launch traced here: 440 us
  waiting for transfers between devices  133 us (30%)
  Pallas kernels  130 us (29%)
  blocking collectives  119 us (27%)
  local copies, waits for them, and re-layouts  23 us (5%)
  between operations  16.5 us (4%)
  starting transfers between devices  12.3 us (3%)
  other arithmetic  5.85 us (1%)
    psum x1, waiting for transfers between devices, shards(): conv, heads = lax.psum((conv, heads), ('group', 'resp'))  85.1 us
    all_gather x1, blocking collectives, shards(): small = lax.all_gather(small, 'resp')  82.4 us
    pallas_call x1, Pallas kernels, response_mid(): pl.pallas_call(resp_mid_kernel, grid=(G,), in_specs=[SMEM, pl.BlockSpec((...  65.7 us
    all_to_all x1, waiting for transfers between devices, shards(): d_states = lax.all_to_all(d_states, 'resp', 0, 0)  47.6 us
    psum x1, blocking collectives, shards(): conv, heads = lax.psum((conv, heads), ('group', 'resp'))  37.1 us
    pallas_call x1, Pallas kernels, prompt_grad(): pl.pallas_call(prompt_grad_kernel, out_shape=(sds((PAD, width + N), f32),...  28.8 us
    pallas_call x1, Pallas kernels, prompt_state(): pl.pallas_call(prompt_state_kernel, out_shape=(sds((N, width), bf16), sds...  16.2 us
    unnamed x58, local copies, waits for them, and re-layouts  12.1 us
  transfers between devices with their start and end apart: 4, of which 2 were waited for; matrix products, arithmetic and copies ran while one was open for 2% of the time, Pallas kernels for 28%

profile of v1, /device:TPU:0, one launch (start us, length us, event | category | flops | bytes accessed | tf_op | source)
XLA Modules:
  0.0 440.3 jit_solution(11558569568607296368)
XLA Ops:
  7.2 1.7 slice.63
  8.9 1.0 slice.64
  9.9 0.2 copy.44
  10.1 0.2 reshape.98
  10.4 0.2 copy.41
  10.7 1.8 fusion.1
  12.4 7.4 %all-to-all-start = ((bf16[8,128,1408]{2,1,0:T(8,128)(2,1)}), bf16[8,128,1408]{2,1,0:T(8,128)(2,1)}, u32[]{:S(2)}, u32[]{:S(2)}) async-start(bf16[8,128,1408]{2,1,0:T(8,128)(2,1)} %fusion.1), calls=%async_computation | async-start | bytes 5767168 | tf_op jit(solution)/shard_map/all_to_all | solution.py:687
  19.9 1.0 slice.46
  20.9 0.1 convert_reduce_fusion.3
  21.0 0.6 slice.52
  21.6 0.7 fusion.4
  22.3 0.3 copy.40
  23.6 0.1 maximum_maximum_fusion
  23.7 82.4 %all-gather = bf16[2048,128]{1,0:T(8,128)(2,1)S(1)} all-gather(bf16[256,128]{1,0:T(8,128)(2,1)S(1)} %maximum_maximum_fusion), channel_id=2, replica_groups=mesh['group'=4,'resp'=8] {'resp'}, dimensions={0}, use_global_device_ids=true | all-gather | bytes 589824 | tf_op jit(solution)/shard_map/all_gather | solution.py:672
  106.8 0.6 convert_reduce_fusion.4
  108.1 0.5 resp_steps.1
  108.8 10.4 %resp_state.1 = (bf16[8,256,1024]{2,1,0:T(8,128)(2,1)}, bf16[256,8192]{1,0:T(8,128)(2,1)}, bf16[256,1024]{1,0:T(8,128)(2,1)S(1)}) custom-call(f32[1,1]{1,0:T(1,128)} %bitcast.7.adv, bf16[256,10240]{1,0:T(8,128)(2,1)} %bitcast.41, f32[8,10240]{1,0:T(8,128)S(1)} %pad_convert_fusion.1.tail_c.tail_x.tail_b, f32[8,10240]{1,0:T(8,128)S(1)} %select_maximum_fusion.wb_c.wb_x.wb_b, ...), custom_call_target="tpu_custom_call" | custom-call | flops 1073741824 | bytes 14680064 | tf_op jit(solution)/shard_map/resp_state/pallas_call | solution.py:455
  119.4 4.6 %all-to-all-start.1 = ((bf16[8,256,1024]{2,1,0:T(8,128)(2,1)}), bf16[8,256,1024]{2,1,0:T(8,128)(2,1)}, u32[]{:S(2)}, u32[]{:S(2)}) async-start(bf16[8,256,1024]{2,1,0:T(8,128)(2,1)} %get-tuple-element.37), calls=%async_computation.1 | async-start | bytes 8388608 | tf_op jit(solution)/shard_map/all_to_all | solution.py:708
  124.2 16.2 %prompt_state.1 = (bf16[256,1024]{1,0:T(8,128)(2,1)}, f32[1024,128]{1,0:T(8,128)S(1)}, f32[1024,128]{1,0:T(8,128)S(1)}) custom-call(bf16[1024,1408]{1,0:T(8,128)(2,1)} %bitcast.20.v, f32[1024,8]{1,0:T(8,128)S(1)} %pad_convert_fusion.masks, f32[8,1280]{1,0:T(8,128)S(1)} %pad_maximum_fusion.2.wb, f32[8,128]{1,0:T(8,128)S(1)} %pad.35.hp), custom_call_target="tpu_custom_call" | custom-call | flops 536870912 | bytes 4194304 | tf_op jit(solution)/shard_map/prompt_state/pallas_call | solution.py:591
  140.4 0.8 copy-done
  141.2 0.2 all-reduce.8.cloned.1.call-start
  141.5 1.0 copy.35
  142.7 1.0 copy-done.2
  143.8 0.9 copy-done.11
  144.7 0.9 copy-done.20
  145.6 65.7 %resp_mid.1 = (f32[8,8192]{1,0:T(8,128)S(1)}, f32[8,1024]{1,0:T(8,128)S(1)}, f32[256,1024]{1,0:T(8,128)S(1)}, f32[256,128]{1,0:T(8,128)S(1)}, f32[256,128]{1,0:T(8,128)S(1)}) custom-call(s32[1,1]{1,0:T(1,128)S(6)} %copy.49.len_ref, bf16[256,10240]{1,0:T(8,128)(2,1)} %bitcast.42, bf16[256,10240]{1,0:T(8,128)(2,1)} %bitcast.43, ...), custom_call_target="tpu_custom_call" | custom-call | flops 12884901888 | bytes 12582912 | tf_op jit(solution)/shard_map/resp_mid/pallas_call | solution.py:487
  211.3 0.6 copy-done.6
  212.0 0.6 copy-done.8
  212.6 0.6 copy-done.16
  213.2 0.7 copy-done.3
  214.0 0.7 reshape_squeeze.8
  214.7 1.5 reduce_sum.63
  216.2 47.6 %all-to-all-done.1.states = bf16[8,256,1024]{2,1,0:T(8,128)(2,1)} async-done(((bf16[8,256,1024]{2,1,0:T(8,128)(2,1)}), bf16[8,256,1024]{2,1,0:T(8,128)(2,1)}, u32[]{:S(2)}, u32[]{:S(2)}) %all-to-all-start.1) | async-done | bytes 4194336 | tf_op jit(solution)/shard_map/all_to_all | solution.py:708
  263.8 1.0 copy-done.1
  264.9 0.7 copy-done.13
  265.6 28.8 %prompt_grad.1 = (f32[8,1280]{1,0:T(8,128)S(1)}, f32[8,128]{1,0:T(8,128)S(1)}) custom-call(bf16[1024,1408]{1,0:T(8,128)(2,1)} %bitcast.20.v, f32[1024,8]{1,0:T(8,128)S(1)} %pad_convert_fusion.masks, f32[8,1280]{1,0:T(8,128)S(1)} %pad_maximum_fusion.2.wb, f32[8,128]{1,0:T(8,128)S(1)} %copy-done.13, f32[1024,128]{1,0:T(8,128)S(1)} %get-tuple-element.35.weight, ...), custom_call_target="tpu_custom_call" | custom-call | flops 1073741824 | bytes 8388608 | tf_op jit(solution)/shard_map/prompt_grad/pallas_call | solution.py:611
  294.4 0.6 copy-done.18
  295.0 0.9 copy-done.7
  295.9 0.9 copy-done.9
  296.8 0.7 copy-done.15
  297.5 8.7 %resp_end.1 = (f32[8,1024]{1,0:T(8,128)S(1)}, f32[8,128]{1,0:T(8,128)S(1)}) custom-call(bf16[256,10240]{1,0:T(8,128)(2,1)} %bitcast.44, f32[8,10240]{1,0:T(8,128)S(1)} %pad_convert_fusion.1.tail_c.tail_x.tail_b, f32[8,10240]{1,0:T(8,128)S(1)} %select_maximum_fusion.wb_c.wb_x.wb_b, bf16[256,1024]{1,0:T(8,128)(2,1)S(1)} %get-tuple-element.23.c_act, ...), custom_call_target="tpu_custom_call" | custom-call | flops 2147483648 | bytes 12582912 | tf_op jit(solution)/shard_map/resp_end/pallas_call | solution.py:555
  306.3 0.7 copy-done.21
  307.1 0.8 fusion.3
  307.9 0.2 dynamic_update_slice.11
  308.1 37.1 %psum.15 = f32[3,128]{1,0:T(4,128)} all-reduce(f32[3,128]{1,0:T(4,128)S(1)} %dynamic_update_slice.11), channel_id=1, replica_groups=mesh['group'=4,'resp'=8] {'group','resp'}, use_global_device_ids=true, to_apply=%region_7.8 | all-reduce | flops 384 | bytes 3072 | tf_op jit(solution)/shard_map/psum | solution.py:730
  345.1 85.1 %all-reduce.8.cloned.1.call-done = f32[5,10240]{1,0:T(8,128)} async-done(((f32[5,10240]{1,0:T(8,128)}), f32[5,10240]{1,0:T(8,128)}) %all-reduce.8.cloned.1.call-update) | async-done | bytes 204816 | tf_op jit(solution)/shard_map/psum | solution.py:730
  430.2 1.7 slice.65
  431.8 1.6 slice.66
  (81 shorter events, 1.4 us)
Async XLA Ops:
  7.2 3.1 copy-start.24
  12.4 8.5 %copy-start.27 = (s32[1,4]{1,0:T(1,128)S(1)}, s32[1,4]{1,0:T(1,128)}, u32[]{:S(2)}) copy-start(s32[1,4]{1,0:T(1,128)} %param.13) | copy-start | bytes 52
  12.4 95.7 %copy-start.25 = (f32[3,128]{1,0:T(4,128)S(1)}, f32[3,128]{1,0:T(4,128)}, u32[]{:S(2)}) copy-start(f32[3,128]{1,0:T(4,128)} %param.21) | copy-start | bytes 4612
  12.4 95.7 %copy-start.5 = (bf16[1,1,256,128]{3,2,1,0:T(8,128)(2,1)S(1)}, bf16[1,1,256,128]{3,2,1,0:T(8,128)(2,1)}, u32[]{:S(2)}) copy-start(bf16[1,1,256,128]{3,2,1,0:T(8,128)(2,1)} %param.15) | copy-start | bytes 196612
  12.4 96.3 %copy-start.22 = (f32[4,10240]{1,0:T(4,128)S(1)}, f32[4,10240]{1,0:T(4,128)}, u32[]{:S(2)}) copy-start(f32[4,10240]{1,0:T(4,128)} %param.19) | copy-start | bytes 491524
  12.4 96.3 %copy-start.23 = (f32[10240]{0:T(1024)S(1)}, f32[10240]{0:T(1024)}, u32[]{:S(2)}) copy-start(f32[10240]{0:T(1024)} %param.20) | copy-start | bytes 122884
  12.4 107.0 %all-to-all-start = ((bf16[8,128,1408]{2,1,0:T(8,128)(2,1)}), bf16[8,128,1408]{2,1,0:T(8,128)(2,1)}, u32[]{:S(2)}, u32[]{:S(2)}) async-start(bf16[8,128,1408]{2,1,0:T(8,128)(2,1)} %fusion.1), calls=%async_computation | async-start | bytes 5767168 | tf_op jit(solution)/shard_map/all_to_all | solution.py:687
  108.1 11.2 %copy-start.14 = (f32[8,128]{1,0:T(8,128)}, f32[8,128]{1,0:T(8,128)S(1)}, u32[]{:S(2)}) copy-start(f32[8,128]{1,0:T(8,128)S(1)} %pad.31.hp) | copy-start | bytes 12292
  108.6 10.6 %copy-start.19 = (f32[128,256]{1,0:T(8,128)}, f32[128,256]{1,0:T(8,128)S(1)}, u32[]{:S(2)}) copy-start(f32[128,256]{1,0:T(8,128)S(1)} %get-tuple-element.26) | copy-start | bytes 393220
  108.6 32.8 %copy-start.10 = (f32[256,128]{1,0:T(8,128)}, f32[256,128]{1,0:T(8,128)S(1)}, u32[]{:S(2)}) copy-start(f32[256,128]{1,0:T(8,128)S(1)} %get-tuple-element.25.cum) | copy-start | bytes 393220
  119.4 144.4 %all-to-all-start.1 = ((bf16[8,256,1024]{2,1,0:T(8,128)(2,1)}), bf16[8,256,1024]{2,1,0:T(8,128)(2,1)}, u32[]{:S(2)}, u32[]{:S(2)}) async-start(bf16[8,256,1024]{2,1,0:T(8,128)(2,1)} %get-tuple-element.37), calls=%async_computation.1 | async-start | bytes 8388608 | tf_op jit(solution)/shard_map/all_to_all | solution.py:708
  124.0 170.9 %all-gather.4.cloned.1.call-start = ((), (), s32[]{:S(2)}) async-start(), calls=%async_computation.3 | async-start | bytes 4718592 | tf_op jit(solution)/shard_map/all_gather | solution.py:707
  124.2 16.2 %copy-start.12 = (f32[8,128]{1,0:T(8,128)}, f32[8,128]{1,0:T(8,128)S(1)}, u32[]{:S(2)}) copy-start(f32[8,128]{1,0:T(8,128)S(1)} %pad.35.hp) | copy-start | bytes 12292
  140.4 0.8 copy-start
  141.2 289.0 %all-reduce.8.cloned.1.call-start = ((), (), s32[]{:S(2)}) async-start(), calls=%async_computation.2 | async-start | bytes 655360 | tf_op jit(solution)/shard_map/psum | solution.py:730
  142.7 1.0 copy-start.2
  143.8 0.9 copy-start.11
  144.7 0.9 copy-start.20
  211.3 0.7 copy-start.6
  212.0 0.6 copy-start.8
  212.6 0.6 copy-start.16
  213.2 0.7 copy-start.3
  263.8 1.0 copy-start.1
  264.9 0.7 copy-start.13
  294.4 0.6 copy-start.18
  295.0 0.9 copy-start.7
  295.9 0.9 copy-start.9
  296.8 0.7 copy-start.15
  297.5 8.8 %copy-start.4 = (f32[8,8192]{1,0:T(8,128)S(1)}, f32[8,8192]{1,0:T(8,128)}, u32[]{:S(2)}) copy-start(f32[8,8192]{1,0:T(8,128)} %copy-done.3) | copy-start | bytes 786436
  297.5 8.8 %copy-start.17 = (f32[8,1024]{1,0:T(8,128)S(1)}, f32[8,1024]{1,0:T(8,128)}, u32[]{:S(2)}) copy-start(f32[8,1024]{1,0:T(8,128)} %copy-done.16) | copy-start | bytes 98308
  297.5 9.6 %copy-start.26 = (f32[128]{0:T(128)S(1)}, f32[128]{0:T(128)}, u32[]{:S(2)}) copy-start(f32[128]{0:T(128)} %reduce_sum.63) | copy-start | bytes 1540
  306.3 0.7 copy-start.21
Sparse Core Ops, SparseCore 0:
  141.3 122.9 all-gather.3
  307.2 122.9 all-reduce.7

commit v2 on v1

--- a/solution.py
+++ b/solution.py
@@ -157,12 +157,13 @@
 
 
 def resp_mid_kernel(
-    len_ref, u_x, u_b, tail_x, tail_b, wb_x, wb_b, c_act, dy, step, cum, cum4, cum_t4, skip,
+    base, len_ref, u_x, u_b, tail_x, tail_b, wb_x, wb_b, c_act, dy, step, cum, cum4, cum_t4, skip,
     grad_x, grad_b, dc, row_out, col_out,
     ext, ext_b, x_s, xs_s, b_s, dym, slope, slope_b, step_e, y_s, t_s,
     a1, bm, sw_e, u_off, y_off, z_hi, z_lo,
 ):
-    g = pl.program_id(0)
+    step_no = pl.program_id(0)
+    g = step_no + base
     rows = u_x.shape[0]
     half = rows // 2
     conv_forward(u_x, tail_x, wb_x, ext, x_s, slope, rows, GX)
@@ -271,19 +272,19 @@
     lane_loop(GX, finish)
     col_sum = head_sums(z_hi[...], z_lo[...], ind)
 
-    @pl.when(g == 0)
+    @pl.when(step_no == 0)
     def _():
         row_out[...] = row_sum
         col_out[...] = col_sum
 
-    @pl.when(g > 0)
+    @pl.when(step_no > 0)
     def _():
         row_out[...] += row_sum
         col_out[...] += col_sum
 
 
 def resp_end_kernel(
-    u_c, tail_c, wb_c, c_act, weighted, start, dc, row_in, col_in, step, dt, hp,
+    u_c, tail_c, wb_c, c_act, weighted, start, dc, row_a, row_b, col_a, col_b, step, dt, hp,
     grad_c, grad_h, ext, c_s, slope, total,
 ):
     g = pl.program_id(0)
@@ -294,7 +295,7 @@
 
     @pl.when(g == 0)
     def _():
-        total[...] = row_in[...] - col_in[...]
+        total[...] = (row_a[...] + row_b[...]) - (col_a[...] + col_b[...])
 
     for s in range(per):
         a = weighted[:, s * width : (s + 1) * width]
@@ -311,7 +312,7 @@
         d_log = tri_sum(triangle(rows, lambda i, j: j >= i), total[...])
         rate = -jnp.exp(hp[0:1])
         s = step[...]
-        d_step = col_in[...] / s + rate * d_log
+        d_step = (col_a[...] + col_b[...]) / s + rate * d_log
         grad_h[...] = jnp.zeros_like(grad_h)
         grad_h[0:1] = jnp.sum(d_log * rate * s, axis=0, keepdims=True)
         grad_h[1:2] = jnp.sum(
@@ -336,7 +337,7 @@
     lane_loop(width, body)
 
 
-def prompt_state_kernel(v, masks, wb, hp, start, weight, step, ext, act, acc):
+def prompt_state_kernel(v, masks, wb, hp, earlier_out, start, weight, step, ext, act, acc):
     rows = v.shape[0]
     width = start.shape[1]
     ind = indicator(0, width)
@@ -478,15 +479,16 @@
     )(scale, u, tail, wb, dy, decay_in)
 
 
-def response_mid(length, u, tail, wb, c_act, dy, step, cum, cum4, cum_t4, skip):
+def response_mid(base, count, length, u, tail, wb, c_act, dy, step, cum, cum4, cum_t4, skip):
     rows = u.shape[0]
     half = rows // 2
-    x_at = lambda g: (0, g)
-    b_at = lambda g: (0, XC // N + g)
+    x_at = lambda g: (0, base + g)
+    b_at = lambda g: (0, XC // N + base + g)
+    out_at = lambda g: (0, g)
     v = pltpu.VMEM
     return pl.pallas_call(
-        resp_mid_kernel,
-        grid=(G,),
+        functools.partial(resp_mid_kernel, base),
+        grid=(count,),
         in_specs=[
             SMEM,
             pl.BlockSpec((rows, GX), x_at),
@@ -499,21 +501,21 @@
             pl.BlockSpec((rows, GX), x_at),
             whole((rows, H)),
             whole((rows, H)),
-            pl.BlockSpec((1, rows, HG), lambda g: (g, 0, 0)),
-            pl.BlockSpec((1, HG, rows), lambda g: (g, 0, 0)),
+            pl.BlockSpec((1, rows, HG), lambda g: (base + g, 0, 0)),
+            pl.BlockSpec((1, HG, rows), lambda g: (base + g, 0, 0)),
             pl.BlockSpec((1, GX), x_at),
         ],
         out_specs=[
-            pl.BlockSpec((PAD, GX), x_at),
-            pl.BlockSpec((PAD, N), x_at),
-            pl.BlockSpec((rows, N), x_at),
+            pl.BlockSpec((PAD, GX), out_at),
+            pl.BlockSpec((PAD, N), out_at),
+            pl.BlockSpec((rows, N), out_at),
             whole((rows, H)),
             whole((rows, H)),
         ],
         out_shape=(
-            sds((PAD, XC), f32),
-            sds((PAD, G * N), f32),
-            sds((rows, G * N), f32),
+            sds((PAD, count * GX), f32),
+            sds((PAD, count * N), f32),
+            sds((rows, count * N), f32),
             sds((rows, H), f32),
             sds((rows, H), f32),
         ),
@@ -539,13 +541,13 @@
         ],
         compiler_params=params("arbitrary"),
         cost_estimate=pl.CostEstimate(
-            flops=12 * 2**30, bytes_accessed=12 * 2**20, transcendentals=rows * half * H
+            flops=count * 8 * 2**30, bytes_accessed=count * 3 * 2**20, transcendentals=rows * half * H
         ),
         name="resp_mid",
     )(length, u, u, tail, tail, wb, wb, c_act, dy, step, cum, cum4, cum_t4, skip)
 
 
-def response_end(u, tail, wb, c_act, weighted, start, dc, row_in, col_in, step, dt, hp):
+def response_end(u, tail, wb, c_act, weighted, start, dc, rows_in, cols_in, step, dt, hp):
     rows = u.shape[0]
     n, _, width = start.shape
     per = n // G
@@ -567,6 +569,8 @@
             whole((rows, H)),
             whole((rows, H)),
             whole((rows, H)),
+            whole((rows, H)),
+            whole((rows, H)),
             whole((PAD, H)),
         ],
         out_specs=[pl.BlockSpec((PAD, N), g_at), whole((PAD, H))],
@@ -582,14 +586,15 @@
             flops=4 * rows * N * XC, bytes_accessed=12 * 2**20, transcendentals=rows * G * N
         ),
         name="resp_end",
-    )(u, tail, wb, c_act, weighted, start, dc, row_in, col_in, step, dt, hp)
-
-
-def prompt_state(v, masks, wb, hp, width):
+    )(u, tail, wb, c_act, weighted, start, dc, *rows_in, *cols_in, step, dt, hp)
+
+
+def prompt_state(v, masks, wb, hp, earlier_out, width):
     rows = v.shape[0]
     s = pltpu.VMEM
     return pl.pallas_call(
         prompt_state_kernel,
+        in_specs=[pl.BlockSpec()] * 4 + [pl.BlockSpec(memory_space=pl.ANY)],
         out_shape=(sds((N, width), bf16), sds((rows, LANES), f32), sds((rows, LANES), f32)),
         scratch_shapes=[
             s((PAD + RB, width + N), f32),
@@ -601,7 +606,7 @@
             flops=2 * rows * N * width, bytes_accessed=4 * 2**20, transcendentals=rows * width
         ),
         name="prompt_state",
-    )(v, masks, wb, hp)
+    )(v, masks, wb, hp, earlier_out)
 
 
 def prompt_grad(v, masks, wb, hp, weight, step, states):
@@ -643,6 +648,15 @@
     return jnp.pad(a, ((0, PAD - a.shape[0]), (0, 0)))
 
 
+def sum_over_all(flat):
+    axes = ("group", "resp")
+    devices = lax.axis_size(axes)
+    rows = -(-flat.size // (devices * LANES))
+    flat = jnp.pad(flat, (0, devices * rows * LANES - flat.size)).reshape(devices, rows, LANES)
+    mine = jnp.sum(lax.all_to_all(flat, axes, 0, 0), axis=0)
+    return lax.all_gather(mine, axes).reshape(-1)
+
+
 def shards(
     prompt_in, prompt_dt, doc_starts, resp_in, resp_dt, resp_len, upstream, reward,
     conv_w, conv_b, head_params,
@@ -670,10 +684,6 @@
         ]
     )
     small = lax.all_gather(small, "resp")
-    tail_rows = small[n - 1, :tail_size].reshape(K - 1, -1).astype(f32)
-    tail = jnp.pad(tail_rows, ((PAD - K + 1, 0), (0, 0)))
-    rewards = jnp.sum(small[:, tail_size : tail_size + 3, 0].astype(f32), axis=1)
-    scale = (r - jnp.sum(rewards) / n) / slots
     wb = pad_rows(jnp.concatenate([conv_w, conv_b[None]], axis=0))
     hp = pad_rows(head_params)
 
@@ -684,9 +694,13 @@
     dt_parts = jnp.pad(
         dt_in.reshape(block, n, hs).transpose(1, 0, 2), ((0, 0), (0, 0), (0, LANES - hs))
     )
-    v = lax.all_to_all(
-        jnp.concatenate([x_parts, b_parts, dt_parts], axis=2), "resp", 0, 0
-    ).reshape(n * block, width + N + LANES)
+    parts = jnp.concatenate([x_parts, b_parts, dt_parts], axis=2)
+    parts, small = lax.optimization_barrier((parts, small))
+    v = lax.all_to_all(parts, "resp", 0, 0).reshape(n * block, width + N + LANES)
+    tail_rows = small[n - 1, :tail_size].reshape(K - 1, -1).astype(f32)
+    tail = jnp.pad(tail_rows, ((PAD - K + 1, 0), (0, 0)))
+    rewards = jnp.sum(small[:, tail_size : tail_size + 3, 0].astype(f32), axis=1)
+    scale = (r - jnp.sum(rewards) / n) / slots
     masks = prompt_masks(doc_starts[0], n * block)
     my_group = me // per
     wb_mine = jnp.concatenate(
@@ -703,18 +717,26 @@
     d_states, weighted, c_act = response_state(
         n, scale.reshape(1, 1), u, tail, wb, dy, decay_in
     )
-    start_mine, weight, p_step = prompt_state(v, masks, wb_mine, hp_mine, width)
-    start = lax.all_gather(start_mine, "resp")
     d_states = lax.all_to_all(d_states, "resp", 0, 0)
 
     cum4 = cum.reshape(slots, G, HG).transpose(1, 0, 2)
     skip = jnp.repeat(head_params[2], PS)[None, :]
-    grad_x, grad_b, dc, row_in, col_in = response_mid(
-        length, u, tail, wb, c_act, dy, step, cum, cum4, cum_t.reshape(G, HG, slots), skip
-    )
+
+    def mid(base, count):
+        return response_mid(
+            base, count, length, u, tail, wb, c_act, dy, step, cum, cum4,
+            cum_t.reshape(G, HG, slots), skip,
+        )
+
+    first = mid(0, G // 2)
+    start_mine, weight, p_step = prompt_state(v, masks, wb_mine, hp_mine, first[1], width)
+    start = lax.all_gather(start_mine, "resp")
+    second = mid(G // 2, G - G // 2)
+    grad_x, grad_b, dc = (jnp.concatenate(ab, axis=1) for ab in zip(first[:3], second[:3]))
+    rows_in, cols_in = zip(first[3:], second[3:])
     p_grad, p_heads = prompt_grad(v, masks, wb_mine, hp_mine, weight, p_step, d_states)
     grad_c, r_heads = response_end(
-        u, tail, wb, c_act, weighted, start, dc, row_in, col_in, step, dt, hp
+        u, tail, wb, c_act, weighted, start, dc, rows_in, cols_in, step, dt, hp
     )
 
     conv = jnp.concatenate([grad_x, grad_b, grad_c], axis=1)[: K + 1] * scale
@@ -727,8 +749,10 @@
     heads = jnp.concatenate([r_heads[:2], d_skip[None]], axis=0) * scale
     mine = lax.dynamic_slice(heads, (0, me * hs), (2, hs)) + p_heads[:2, :hs]
     heads = lax.dynamic_update_slice(heads, mine, (0, me * hs))
-    conv, heads = lax.psum((conv, heads), ("group", "resp"))
-    return conv[:K], conv[K], heads
+    flat = sum_over_all(jnp.concatenate([conv.reshape(-1), heads.reshape(-1)]))
+    at_heads = conv.size
+    conv = flat[:at_heads].reshape(conv.shape)
+    return conv[:K], conv[K], flat[at_heads : at_heads + heads.size].reshape(heads.shape)
 
 
 def solution(mesh):

time: 442 us -> 393 us (0.89)
  waiting for transfers between devices: 133 us -> 92.9 us
  blocking collectives: 119 us -> 112 us
    psum x1 -> x0, waiting for transfers between devices: 85.1 us -> none  [shards(): conv, heads = lax.psum((conv, heads), ('group', 'resp'))]
    all_gather x0 -> x1, blocking collectives: none -> 66.2 us  [sum_over_all(): return lax.all_gather(mine, axes).reshape(-1)]
    all_gather x1, blocking collectives: 82.4 us -> 33 us  [shards(): small = lax.all_gather(small, 'resp')]
    all_to_all x1, waiting for transfers between devices: 47.6 us -> 84.9 us  [shards(): d_states = lax.all_to_all(d_states, 'resp', 0, 0)]
    psum x1 -> x0, blocking collectives: 37.1 us -> none  [shards(): conv, heads = lax.psum((conv, heads), ('group', 'resp'))]
    all_to_all x0 -> x1, blocking collectives: none -> 12.9 us  [sum_over_all(): mine = jnp.sum(lax.all_to_all(flat, axes, 0, 0), axis=0)]
    all_to_all x1, waiting for transfers between devices: 0.01 us -> 8.01 us  [shards(): lax.all_to_all(parts, 'resp', 0, 0).reshape(n * block, width + N + LANES)]
    pallas_call x2 -> x3, Pallas kernels: 81.9 us -> 83.5 us  [the longest x2 67.3 us: response_mid(): pl.pallas_call(functools.partial(resp_mid_kernel, base), grid=(count,), i...]
  transfers between devices with their start and end apart: 4 -> 3, of which waited for: 2 -> 2; matrix products, arithmetic and copies ran while one was open for 2% -> 1% of each run, Pallas kernels for 28% -> 31%
where the time goes in v2:
time: 393 us; the launch traced here: 392 us
  Pallas kernels  132 us (34%)
  blocking collectives  112 us (28%)
  waiting for transfers between devices  92.9 us (24%)
  local copies, waits for them, and re-layouts  21.7 us (6%)
  between operations  16.6 us (4%)
  starting transfers between devices  10.7 us (3%)
  other arithmetic  6.44 us (2%)
    all_to_all x1, waiting for transfers between devices, shards(): d_states = lax.all_to_all(d_states, 'resp', 0, 0)  84.9 us
    pallas_call x2, Pallas kernels, response_mid(): pl.pallas_call(functools.partial(resp_mid_kernel, base), grid=(count,), i...  67.3 us
    all_gather x1, blocking collectives, sum_over_all(): return lax.all_gather(mine, axes).reshape(-1)  66.2 us
    all_gather x1, blocking collectives, shards(): small = lax.all_gather(small, 'resp')  33 us
    pallas_call x1, Pallas kernels, prompt_grad(): pl.pallas_call(prompt_grad_kernel, out_shape=(sds((PAD, width + N), f32),...  28.8 us
    pallas_call x1, Pallas kernels, prompt_state(): pl.pallas_call(prompt_state_kernel, in_specs=[pl.BlockSpec()] * 4 + [pl.B...  16.2 us
    unnamed x63, local copies, waits for them, and re-layouts  13.6 us
    all_to_all x1, blocking collectives, sum_over_all(): mine = jnp.sum(lax.all_to_all(flat, axes, 0, 0), axis=0)  12.9 us
  transfers between devices with their start and end apart: 3, of which 2 were waited for; matrix products, arithmetic and copies ran while one was open for 1% of the time, Pallas kernels for 31%

profile of v2, /device:TPU:0, one launch (start us, length us, event | category | flops | bytes accessed | tf_op | source)
XLA Modules:
  0.0 392.4 jit_solution(9658524826792692847)
XLA Ops:
  7.2 1.0 slice.63
  8.1 1.0 slice.83
  9.1 1.7 slice.82
  12.5 33.0 %all-gather = bf16[2048,128]{1,0:T(8,128)(2,1)S(1)} all-gather(bf16[256,128]{1,0:T(8,128)(2,1)S(1)} %maximum_maximum_fusion), channel_id=2, replica_groups=mesh['group'=4,'resp'=8] {'resp'}, dimensions={0}, use_global_device_ids=true | all-gather | bytes 589824 | tf_op jit(solution)/shard_map/all_gather | solution.py:686
  45.7 1.8 fusion.1
  47.5 5.8 %all-to-all-start = ((bf16[8,128,1408]{2,1,0:T(8,128)(2,1)}), bf16[8,128,1408]{2,1,0:T(8,128)(2,1)}, u32[]{:S(2)}, u32[]{:S(2)}) async-start(bf16[8,128,1408]{2,1,0:T(8,128)(2,1)} %fusion.1), calls=%async_computation | async-start | bytes 5767168 | tf_op jit(solution)/shard_map/all_to_all | solution.py:699
  53.5 0.6 slice.67
  54.0 0.7 fusion.4
  55.7 0.3 copy.40
  56.0 0.5 resp_steps.1
  56.6 0.2 copy.39
  56.9 0.6 convert_reduce_fusion.4
  58.3 10.4 %resp_state.1 = (bf16[8,256,1024]{2,1,0:T(8,128)(2,1)}, bf16[256,8192]{1,0:T(8,128)(2,1)}, bf16[256,1024]{1,0:T(8,128)(2,1)S(1)}) custom-call(f32[1,1]{1,0:T(1,128)} %bitcast.13.adv, bf16[256,10240]{1,0:T(8,128)(2,1)} %bitcast.46, f32[8,10240]{1,0:T(8,128)S(1)} %pad_convert_fusion.1.tail_c.tail_x.tail_b, f32[8,10240]{1,0:T(8,128)S(1)} %select_maximum_fusion.wb_c.wb_x.wb_b, ...), custom_call_target="tpu_custom_call" | custom-call | flops 1073741824 | bytes 14680064 | tf_op jit(solution)/shard_map/resp_state/pallas_call | solution.py:456
  68.8 33.7 %resp_mid.2 = (f32[8,4096]{1,0:T(8,128)S(1)}, f32[8,512]{1,0:T(8,128)S(1)}, f32[256,512]{1,0:T(8,128)S(1)}, f32[256,128]{1,0:T(8,128)S(1)}, f32[256,128]{1,0:T(8,128)S(1)}) custom-call(s32[1,1]{1,0:T(1,128)S(6)} %copy.52.len_ref, bf16[256,10240]{1,0:T(8,128)(2,1)} %bitcast.47, bf16[256,10240]{1,0:T(8,128)(2,1)} %bitcast.48, ...), custom_call_target="tpu_custom_call" | custom-call | flops 17179869184 | bytes 6291456 | tf_op jit(solution)/shard_map/resp_mid/pallas_call | solution.py:489
  102.5 0.8 copy-done.2
  103.3 0.6 copy-done.5
  104.0 0.7 copy-done.7
  104.6 8.0 %all-to-all-done = bf16[8,128,1408]{2,1,0:T(8,128)(2,1)} async-done(((bf16[8,128,1408]{2,1,0:T(8,128)(2,1)}), bf16[8,128,1408]{2,1,0:T(8,128)(2,1)}, u32[]{:S(2)}, u32[]{:S(2)}) %all-to-all-start) | async-done | bytes 2883616 | tf_op jit(solution)/shard_map/all_to_all | solution.py:699
  112.6 4.6 %all-to-all-start.1 = ((bf16[8,256,1024]{2,1,0:T(8,128)(2,1)}), bf16[8,256,1024]{2,1,0:T(8,128)(2,1)}, u32[]{:S(2)}, u32[]{:S(2)}) async-start(bf16[8,256,1024]{2,1,0:T(8,128)(2,1)} %get-tuple-element.51), calls=%async_computation.1 | async-start | bytes 8388608 | tf_op jit(solution)/shard_map/all_to_all | solution.py:720
  117.3 0.2 all-gather.6.cloned.1.call-start
  117.6 16.2 %prompt_state.1 = (bf16[256,1024]{1,0:T(8,128)(2,1)}, f32[1024,128]{1,0:T(8,128)S(1)}, f32[1024,128]{1,0:T(8,128)S(1)}) custom-call(bf16[1024,1408]{1,0:T(8,128)(2,1)} %bitcast.20.v, f32[1024,8]{1,0:T(8,128)S(1)} %pad_convert_fusion.masks, f32[8,1280]{1,0:T(8,128)S(1)} %pad_maximum_fusion.1.wb, f32[8,128]{1,0:T(8,128)S(1)} %pad.39.hp, ...), custom_call_target="tpu_custom_call" | custom-call | flops 536870912 | bytes 4194304 | tf_op jit(solution)/shard_map/prompt_state/pallas_call | solution.py:595
  133.8 0.8 copy-done
  134.6 0.9 copy-done.19
  135.5 33.6 %resp_mid.3 = (f32[8,4096]{1,0:T(8,128)S(1)}, f32[8,512]{1,0:T(8,128)S(1)}, f32[256,512]{1,0:T(8,128)S(1)}, f32[256,128]{1,0:T(8,128)S(1)}, f32[256,128]{1,0:T(8,128)S(1)}) custom-call(s32[1,1]{1,0:T(1,128)S(6)} %copy.52.len_ref, bf16[256,10240]{1,0:T(8,128)(2,1)} %bitcast.49, bf16[256,10240]{1,0:T(8,128)(2,1)} %bitcast.50, ...), custom_call_target="tpu_custom_call" | custom-call | flops 17179869184 | bytes 6291456 | tf_op jit(solution)/shard_map/resp_mid/pallas_call | solution.py:489
  169.2 0.8 copy-done.3
  170.0 0.7 copy-done.9
  170.6 0.6 copy-done.11
  171.4 0.6 reduce_sum.72
  172.1 0.7 copy-done.20
  172.9 1.3 pad_maximum_fusion.dc
  174.1 84.9 %all-to-all-done.1.states = bf16[8,256,1024]{2,1,0:T(8,128)(2,1)} async-done(((bf16[8,256,1024]{2,1,0:T(8,128)(2,1)}), bf16[8,256,1024]{2,1,0:T(8,128)(2,1)}, u32[]{:S(2)}, u32[]{:S(2)}) %all-to-all-start.1) | async-done | bytes 4194336 | tf_op jit(solution)/shard_map/all_to_all | solution.py:720
  259.0 1.0 copy-done.1
  260.1 0.7 copy-done.14
  260.8 28.8 %prompt_grad.1 = (f32[8,1280]{1,0:T(8,128)S(1)}, f32[8,128]{1,0:T(8,128)S(1)}) custom-call(bf16[1024,1408]{1,0:T(8,128)(2,1)} %bitcast.20.v, f32[1024,8]{1,0:T(8,128)S(1)} %pad_convert_fusion.masks, f32[8,1280]{1,0:T(8,128)S(1)} %pad_maximum_fusion.1.wb, f32[8,128]{1,0:T(8,128)S(1)} %copy-done.14, f32[1024,128]{1,0:T(8,128)S(1)} %get-tuple-element.49.weight, ...), custom_call_target="tpu_custom_call" | custom-call | flops 1073741824 | bytes 8388608 | tf_op jit(solution)/shard_map/prompt_grad/pallas_call | solution.py:616
  289.6 0.6 copy-done.17
  290.2 0.9 copy-done.6
  291.1 0.9 copy-done.8
  292.0 0.9 copy-done.10
  292.9 0.9 copy-done.12
  293.8 0.7 copy-done.16
  294.5 8.8 %resp_end.1 = (f32[8,1024]{1,0:T(8,128)S(1)}, f32[8,128]{1,0:T(8,128)S(1)}) custom-call(bf16[256,10240]{1,0:T(8,128)(2,1)} %bitcast.51, f32[8,10240]{1,0:T(8,128)S(1)} %pad_convert_fusion.1.tail_c.tail_x.tail_b, f32[8,10240]{1,0:T(8,128)S(1)} %select_maximum_fusion.wb_c.wb_x.wb_b, bf16[256,1024]{1,0:T(8,128)(2,1)S(1)} %get-tuple-element.31.c_act, ...), custom_call_target="tpu_custom_call" | custom-call | flops 2147483648 | bytes 12582912 | tf_op jit(solution)/shard_map/resp_end/pallas_call | solution.py:557
  303.5 0.8 fusion.3
  304.2 0.2 dynamic_update_slice.11
  304.5 12.9 %all_to_all.15 = f32[32,13,128]{2,1,0:T(8,128)S(1)} all-to-all(f32[32,13,128]{2,1,0:T(8,128)S(1)} %reshape.125), channel_id=1, replica_groups=mesh['group'=4,'resp'=8] {'group','resp'}, dimensions={0} | all-to-all | bytes 425984 | tf_op jit(solution)/shard_map/all_to_all | solution.py:656
  317.4 66.2 %all-gather.3 = f32[32,13,128]{2,1,0:T(8,128)S(1)} all-gather(f32[1,13,128]{2,1,0:T(8,128)S(1)} %bitcast.67), channel_id=4, replica_groups=mesh['group'=4,'resp'=8] {'group','resp'}, dimensions={0}, use_global_device_ids=true | all-gather | bytes 219648 | tf_op jit(solution)/shard_map/all_gather | solution.py:657
  383.6 0.6 slice.87
  384.2 0.6 slice_bitcast_fusion
  384.8 0.7 slice.75
  (93 shorter events, 2.4 us)
Async XLA Ops:
  7.2 4.4 %copy-start.24 = (bf16[1,128,128]{2,1,0:T(8,128)(2,1)S(1)}, bf16[1,128,128]{2,1,0:T(8,128)(2,1)}, u32[]{:S(2)}) copy-start(bf16[1,128,128]{2,1,0:T(8,128)(2,1)} %param.12) | copy-start | bytes 98308
  47.4 5.9 %copy-start.27 = (s32[1,4]{1,0:T(1,128)S(1)}, s32[1,4]{1,0:T(1,128)}, u32[]{:S(2)}) copy-start(s32[1,4]{1,0:T(1,128)} %param.13) | copy-start | bytes 52
  47.4 8.0 %copy-start.25 = (f32[3,128]{1,0:T(4,128)S(1)}, f32[3,128]{1,0:T(4,128)}, u32[]{:S(2)}) copy-start(f32[3,128]{1,0:T(4,128)} %param.21) | copy-start | bytes 4612
  47.4 8.5 %copy-start.4 = (bf16[1,1,256,128]{3,2,1,0:T(8,128)(2,1)S(1)}, bf16[1,1,256,128]{3,2,1,0:T(8,128)(2,1)}, u32[]{:S(2)}) copy-start(bf16[1,1,256,128]{3,2,1,0:T(8,128)(2,1)} %param.15) | copy-start | bytes 196612
  47.4 10.7 %copy-start.22 = (f32[4,10240]{1,0:T(4,128)S(1)}, f32[4,10240]{1,0:T(4,128)}, u32[]{:S(2)}) copy-start(f32[4,10240]{1,0:T(4,128)} %param.19) | copy-start | bytes 491524
  47.5 10.7 %copy-start.23 = (f32[10240]{0:T(1024)S(1)}, f32[10240]{0:T(1024)}, u32[]{:S(2)}) copy-start(f32[10240]{0:T(1024)} %param.20) | copy-start | bytes 122884
  47.5 65.2 %all-to-all-start = ((bf16[8,128,1408]{2,1,0:T(8,128)(2,1)}), bf16[8,128,1408]{2,1,0:T(8,128)(2,1)}, u32[]{:S(2)}, u32[]{:S(2)}) async-start(bf16[8,128,1408]{2,1,0:T(8,128)(2,1)} %fusion.1), calls=%async_computation | async-start | bytes 5767168 | tf_op jit(solution)/shard_map/all_to_all | solution.py:699
  55.4 13.3 %copy-start.15 = (f32[8,128]{1,0:T(8,128)}, f32[8,128]{1,0:T(8,128)S(1)}, u32[]{:S(2)}) copy-start(f32[8,128]{1,0:T(8,128)S(1)} %pad.36.hp) | copy-start | bytes 12292
  56.5 12.3 %copy-start.18 = (f32[128,256]{1,0:T(8,128)}, f32[128,256]{1,0:T(8,128)S(1)}, u32[]{:S(2)}) copy-start(f32[128,256]{1,0:T(8,128)S(1)} %get-tuple-element.34) | copy-start | bytes 393220
  102.5 0.8 copy-start.2
  103.3 0.7 copy-start.5
  104.0 0.7 copy-start.7
  112.6 146.4 %all-to-all-start.1 = ((bf16[8,256,1024]{2,1,0:T(8,128)(2,1)}), bf16[8,256,1024]{2,1,0:T(8,128)(2,1)}, u32[]{:S(2)}, u32[]{:S(2)}) async-start(bf16[8,256,1024]{2,1,0:T(8,128)(2,1)} %get-tuple-element.51), calls=%async_computation.1 | async-start | bytes 8388608 | tf_op jit(solution)/shard_map/all_to_all | solution.py:720
  117.3 172.9 %all-gather.6.cloned.1.call-start = ((), (), s32[]{:S(2)}) async-start(), calls=%async_computation.3 | async-start | bytes 4718592 | tf_op jit(solution)/shard_map/all_gather | solution.py:733
  117.6 16.2 %copy-start.13 = (f32[8,128]{1,0:T(8,128)}, f32[8,128]{1,0:T(8,128)S(1)}, u32[]{:S(2)}) copy-start(f32[8,128]{1,0:T(8,128)S(1)} %pad.39.hp) | copy-start | bytes 12292
  133.8 0.8 copy-start
  134.6 0.9 copy-start.19
  169.1 0.8 copy-start.3
  170.0 0.7 copy-start.9
  170.6 0.7 copy-start.11
  172.1 0.7 copy-start.20
  259.0 1.0 copy-start.1
  260.1 0.7 copy-start.14
  289.6 0.6 copy-start.17
  290.2 0.9 copy-start.6
  291.1 0.9 copy-start.8
  292.0 0.9 copy-start.10
  292.9 0.9 copy-start.12
  293.8 0.7 copy-start.16
  294.5 8.8 %copy-start.21 = (f32[8,10240]{1,0:T(8,128)S(1)}, f32[8,10240]{1,0:T(8,128)}, u32[]{:S(2)}) copy-start(f32[8,10240]{1,0:T(8,128)} %copy-done.20) | copy-start | bytes 983044
  294.5 9.0 %copy-start.26 = (f32[128]{0:T(128)S(1)}, f32[128]{0:T(128)}, u32[]{:S(2)}) copy-start(f32[128]{0:T(128)} %reduce_sum.72) | copy-start | bytes 1540
Sparse Core Ops, SparseCore 0:
  134.7 127.0 all-gather.5

commit v3 on v2

--- a/solution.py
+++ b/solution.py
@@ -141,7 +141,9 @@
     decay_in[...] = jnp.where(t < len_ref[0, 0], jnp.exp(c), 0.0)
 
 
-def resp_state_kernel(per, adv, u_c, tail_c, wb_c, dy, decay_in, state, weighted, c_out, ext, c_t):
+def resp_state_kernel(
+    per, side, adv, u_c, tail_c, wb_c, dy, decay_in, kept, sent, weighted, c_out, ext, c_t
+):
     slab = pl.program_id(0)
     rows, width = dy.shape
 
@@ -153,7 +155,15 @@
     ind = indicator(slab * (width // PS), width)
     a = (dy[...].astype(f32) * expand(decay_in[...], ind)).astype(bf16)
     weighted[...] = a
-    state[0] = (dot(c_t[...], a) * adv[0, 0]).astype(bf16)
+    state = (dot(c_t[...], a) * adv[0, 0]).astype(bf16)
+
+    @pl.when(slab % 2 == side[0, 0])
+    def _():
+        kept[0] = state
+
+    @pl.when(slab % 2 != side[0, 0])
+    def _():
+        sent[0] = state
 
 
 def resp_mid_kernel(
@@ -421,6 +431,10 @@
     grad_h[1:2] = d_bias
 
 
+def add_kernel(a, b, earlier_out, out):
+    out[...] = (a[...].astype(f32) + b[...].astype(f32)).astype(bf16)
+
+
 def params(*semantics):
     return pltpu.CompilerParams(vmem_limit_bytes=VMEM_LIMIT, dimension_semantics=semantics or None)
 
@@ -448,7 +462,7 @@
     )(length, dt, hp)
 
 
-def response_state(n, scale, u, tail, wb, dy, decay_in):
+def response_state(n, side, scale, u, tail, wb, dy, decay_in):
     rows = u.shape[0]
     per = n // G
     width = XC // n
@@ -458,6 +472,7 @@
         grid=(n,),
         in_specs=[
             SMEM,
+            SMEM,
             pl.BlockSpec((rows, N), c_at),
             pl.BlockSpec((PAD, N), c_at),
             pl.BlockSpec((PAD, N), c_at),
@@ -465,18 +480,24 @@
             whole((rows, H)),
         ],
         out_specs=[
-            pl.BlockSpec((1, N, width), lambda i: (i, 0, 0)),
+            pl.BlockSpec((1, N, width), lambda i: (i // 2, 0, 0)),
+            pl.BlockSpec((1, N, width), lambda i: (i // 2, 0, 0)),
             pl.BlockSpec((rows, width), lambda i: (0, i)),
             pl.BlockSpec((rows, N), lambda i: (0, i // per)),
         ],
-        out_shape=(sds((n, N, width), bf16), sds((rows, XC), bf16), sds((rows, G * N), bf16)),
+        out_shape=(
+            sds((n // 2, N, width), bf16),
+            sds((n // 2, N, width), bf16),
+            sds((rows, XC), bf16),
+            sds((rows, G * N), bf16),
+        ),
         scratch_shapes=[pltpu.VMEM((PAD + rows, N), f32), pltpu.VMEM((N, rows), bf16)],
         compiler_params=params("arbitrary"),
         cost_estimate=pl.CostEstimate(
             flops=2 * rows * N * XC, bytes_accessed=14 * 2**20, transcendentals=rows * G * N
         ),
         name="resp_state",
-    )(scale, u, tail, wb, dy, decay_in)
+    )(side, scale, u, tail, wb, dy, decay_in)
 
 
 def response_mid(base, count, length, u, tail, wb, c_act, dy, step, cum, cum4, cum_t4, skip):
@@ -589,6 +610,20 @@
     )(u, tail, wb, c_act, weighted, start, dc, *rows_in, *cols_in, step, dt, hp)
 
 
+def add_pairs(a, b, earlier_out):
+    block = pl.BlockSpec((1,) + a.shape[1:], lambda i: (i, 0, 0))
+    return pl.pallas_call(
+        add_kernel,
+        grid=(a.shape[0],),
+        in_specs=[block, block, pl.BlockSpec(memory_space=pl.ANY)],
+        out_specs=block,
+        out_shape=sds(a.shape, bf16),
+        compiler_params=params("arbitrary"),
+        cost_estimate=pl.CostEstimate(flops=a.size, bytes_accessed=6 * a.size, transcendentals=0),
+        name="add_pairs",
+    )(a, b, earlier_out)
+
+
 def prompt_state(v, masks, wb, hp, earlier_out, width):
     rows = v.shape[0]
     s = pltpu.VMEM
@@ -648,13 +683,17 @@
     return jnp.pad(a, ((0, PAD - a.shape[0]), (0, 0)))
 
 
+def to_all(block, axes, devices):
+    return lax.all_to_all(jnp.broadcast_to(block[None], (devices,) + block.shape), axes, 0, 0)
+
+
 def sum_over_all(flat):
     axes = ("group", "resp")
     devices = lax.axis_size(axes)
     rows = -(-flat.size // (devices * LANES))
     flat = jnp.pad(flat, (0, devices * rows * LANES - flat.size)).reshape(devices, rows, LANES)
     mine = jnp.sum(lax.all_to_all(flat, axes, 0, 0), axis=0)
-    return lax.all_gather(mine, axes).reshape(-1)
+    return to_all(mine, axes, devices).reshape(-1)
 
 
 def shards(
@@ -683,7 +722,7 @@
             jnp.zeros((12, LANES), bf16),
         ]
     )
-    small = lax.all_gather(small, "resp")
+    small = to_all(small, "resp", n)
     wb = pad_rows(jnp.concatenate([conv_w, conv_b[None]], axis=0))
     hp = pad_rows(head_params)
 
@@ -714,10 +753,10 @@
 
     length = resp_len.astype(jnp.int32)
     step, cum, cum_t, decay_in = response_steps(length, dt, hp)
-    d_states, weighted, c_act = response_state(
-        n, scale.reshape(1, 1), u, tail, wb, dy, decay_in
+    kept, sent, weighted, c_act = response_state(
+        n, (me % 2).reshape(1, 1), scale.reshape(1, 1), u, tail, wb, dy, decay_in
     )
-    d_states = lax.all_to_all(d_states, "resp", 0, 0)
+    met = lax.ppermute(sent, "resp", [(i, i ^ 1) for i in range(n)])
 
     cum4 = cum.reshape(slots, G, HG).transpose(1, 0, 2)
     skip = jnp.repeat(head_params[2], PS)[None, :]
@@ -729,7 +768,12 @@
         )
 
     first = mid(0, G // 2)
-    start_mine, weight, p_step = prompt_state(v, masks, wb_mine, hp_mine, first[1], width)
+    pair_sums = add_pairs(kept, met, first[1])
+    d_states = lax.all_to_all(
+        pair_sums, "resp", 0, 0,
+        axis_index_groups=[list(range(0, n, 2)), list(range(1, n, 2))],
+    )
+    start_mine, weight, p_step = prompt_state(v, masks, wb_mine, hp_mine, pair_sums, width)
     start = lax.all_gather(start_mine, "resp")
     second = mid(G // 2, G - G // 2)
     grad_x, grad_b, dc = (jnp.concatenate(ab, axis=1) for ab in zip(first[:3], second[:3]))

time: 393 us -> 307 us (0.78)
  blocking collectives: 112 us -> 28.2 us
  waiting for transfers between devices: 92.9 us -> 49.6 us
  local copies, waits for them, and re-layouts: 21.7 us -> 40.5 us
  starting transfers between devices: 10.7 us -> 23.6 us
  other arithmetic: 6.44 us -> 11.1 us
  Pallas kernels: 132 us -> 136 us
    all_gather x2 -> x0, blocking collectives: 99.2 us -> none  [the longest x1 66.2 us: sum_over_all(): return lax.all_gather(mine, axes).reshape(-1)]
    all_to_all x1 -> x2, waiting for transfers between devices: 84.9 us -> 26.3 us  [the longest x1 20.9 us: shards(): lax.all_to_all(pair_sums, 'resp', 0, 0, axis_index_groups=[list(range(0,...]
    ppermute x0 -> x1, waiting for transfers between devices: none -> 23.3 us  [shards(): met = lax.ppermute(sent, 'resp', [(i, i ^ 1) for i in range(n)])]
    unnamed x63 -> x96, local copies, waits for them, and re-layouts: 13.6 us -> 27.2 us
    all_to_all x0 -> x1, blocking collectives: none -> 12.8 us  [to_all(): lax.all_to_all(jnp.broadcast_to(block[None], (devices,) + block.shape), a...]
    all_to_all x1 -> x2, starting transfers between devices: 4.6 us -> 17.3 us  [the longest x1 9.88 us: shards(): lax.all_to_all(pair_sums, 'resp', 0, 0, axis_index_groups=[list(range(0,...]
    all_to_all x1, waiting for transfers between devices: 8.01 us -> 0.01 us  [shards(): lax.all_to_all(parts, 'resp', 0, 0).reshape(n * block, width + N + LANES)]
    pallas_call x0 -> x1, Pallas kernels: none -> 4.29 us  [add_pairs(): pl.pallas_call(add_kernel, grid=(a.shape[0],), in_specs=[block, block, pl...]
  transfers between devices with their start and end apart: 3 -> 5, of which waited for: 2 -> 3; matrix products, arithmetic and copies ran while one was open for 1% -> 7% of each run, Pallas kernels for 31% -> 36%
where the time goes in v3:
time: 307 us; the launch traced here: 305 us
  Pallas kernels  136 us (44%)
  waiting for transfers between devices  49.6 us (16%)
  local copies, waits for them, and re-layouts  40.5 us (13%)
  blocking collectives  28.2 us (9%)
  starting transfers between devices  23.6 us (8%)
  between operations  16.6 us (5%)
  other arithmetic  11.1 us (4%)
    pallas_call x2, Pallas kernels, response_mid(): pl.pallas_call(functools.partial(resp_mid_kernel, base), grid=(count,), i...  67.4 us
    pallas_call x1, Pallas kernels, prompt_grad(): pl.pallas_call(prompt_grad_kernel, out_shape=(sds((PAD, width + N), f32),...  27.4 us
    unnamed x96, local copies, waits for them, and re-layouts  27.2 us
    ppermute x1, waiting for transfers between devices, shards(): met = lax.ppermute(sent, 'resp', [(i, i ^ 1) for i in range(n)])  23.3 us
    all_to_all x1, waiting for transfers between devices, shards(): lax.all_to_all(pair_sums, 'resp', 0, 0, axis_index_groups=[list(range(0,...  20.9 us
    pallas_call x1, Pallas kernels, prompt_state(): pl.pallas_call(prompt_state_kernel, in_specs=[pl.BlockSpec()] * 4 + [pl.B...  16.2 us
    all_to_all x1, blocking collectives, sum_over_all(): mine = jnp.sum(lax.all_to_all(flat, axes, 0, 0), axis=0)  15.3 us
    all_to_all x1, blocking collectives, to_all(): lax.all_to_all(jnp.broadcast_to(block[None], (devices,) + block.shape), a...  12.8 us
  transfers between devices with their start and end apart: 5, of which 3 were waited for; matrix products, arithmetic and copies ran while one was open for 7% of the time, Pallas kernels for 36%

profile of v3, /device:TPU:0, one launch (start us, length us, event | category | flops | bytes accessed | tf_op | source)
XLA Modules:
  0.0 305.2 jit_solution(12375348603536327927)
XLA Ops:
  7.8 1.0 slice.63
  9.2 0.9 broadcast_in_dim.19
  10.1 7.4 %all-to-all-start = ((bf16[8,256,128]{2,1,0:T(8,128)(2,1)}), bf16[8,256,128]{2,1,0:T(8,128)(2,1)}, u32[]{:S(2)}, u32[]{:S(2)}) async-start(bf16[8,256,128]{2,1,0:T(8,128)(2,1)} %broadcast_in_dim.19), calls=%async_computation | async-start | bytes 1048576 | tf_op jit(solution)/shard_map/all_to_all | solution.py:687
  17.5 1.0 slice.80
  18.5 1.7 slice.79
  21.5 1.6 copy.44
  23.8 2.9 fusion.1
  26.7 5.4 %all-to-all-done = bf16[8,256,128]{2,1,0:T(8,128)(2,1)} async-done(((bf16[8,256,128]{2,1,0:T(8,128)(2,1)}), bf16[8,256,128]{2,1,0:T(8,128)(2,1)}, u32[]{:S(2)}, u32[]{:S(2)}) %all-to-all-start) | async-done | bytes 524320 | tf_op jit(solution)/shard_map/all_to_all | solution.py:687
  32.1 4.5 %all-to-all-start.1 = ((bf16[8,128,1408]{2,1,0:T(8,128)(2,1)}), bf16[8,128,1408]{2,1,0:T(8,128)(2,1)}, u32[]{:S(2)}, u32[]{:S(2)}) async-start(bf16[8,128,1408]{2,1,0:T(8,128)(2,1)} %fusion.1), calls=%async_computation.1 | async-start | bytes 5767168 | tf_op jit(solution)/shard_map/all_to_all | solution.py:738
  38.1 0.8 slice.64
  39.0 1.3 convert_reduce_fusion.4
  41.0 11.1 %resp_state.1 = (bf16[4,256,1024]{2,1,0:T(8,128)(2,1)S(1)}, bf16[4,256,1024]{2,1,0:T(8,128)(2,1)}, bf16[256,8192]{1,0:T(8,128)(2,1)}, bf16[256,1024]{1,0:T(8,128)(2,1)S(1)}) custom-call(s32[1,1]{1,0:T(1,128)} %bitcast.12.side, f32[1,1]{1,0:T(1,128)} %bitcast.13.adv, bf16[256,10240]{1,0:T(8,128)(2,1)} %bitcast.43, ...), custom_call_target="tpu_custom_call" | custom-call | flops 1073741824 | bytes 14680064 | tf_op jit(solution)/shard_map/resp_state/pallas_call | solution.py:470
  52.1 1.3 copy-done.1
  53.4 1.8 collective-permute-start
  56.3 33.7 %resp_mid.2 = (f32[8,4096]{1,0:T(8,128)S(1)}, f32[8,512]{1,0:T(8,128)S(1)}, f32[256,512]{1,0:T(8,128)S(1)}, f32[256,128]{1,0:T(8,128)S(1)}, f32[256,128]{1,0:T(8,128)S(1)}) custom-call(s32[1,1]{1,0:T(1,128)S(6)} %copy.52.len_ref, bf16[256,10240]{1,0:T(8,128)(2,1)} %bitcast.44, bf16[256,10240]{1,0:T(8,128)(2,1)} %bitcast.45, ...), custom_call_target="tpu_custom_call" | custom-call | flops 17179869184 | bytes 6291456 | tf_op jit(solution)/shard_map/resp_mid/pallas_call | solution.py:510
  90.1 0.8 copy-done.11
  92.1 23.3 %collective-permute-done.b = bf16[4,256,1024]{2,1,0:T(8,128)(2,1)} collective-permute-done((bf16[4,256,1024]{2,1,0:T(8,128)(2,1)}, bf16[4,256,1024]{2,1,0:T(8,128)(2,1)}, u32[]{:S(2)}, u32[]{:S(2)}) %collective-permute-start) | collective-permute-done | bytes 2097184 | tf_op jit(solution)/shard_map/ppermute | solution.py:759
  115.4 4.3 %add_pairs.1.earlier_out = bf16[4,256,1024]{2,1,0:T(8,128)(2,1)} custom-call(bf16[4,256,1024]{2,1,0:T(8,128)(2,1)} %copy-done.1, bf16[4,256,1024]{2,1,0:T(8,128)(2,1)} %collective-permute-done.b, f32[8,512]{1,0:T(8,128)S(1)} %get-tuple-element.38.earlier_out), custom_call_target="tpu_custom_call" | custom-call | flops 1048576 | bytes 6291456 | tf_op jit(solution)/shard_map/add_pairs/pallas_call | solution.py:615
  119.7 16.2 %prompt_state.1 = (bf16[256,1024]{1,0:T(8,128)(2,1)}, f32[1024,128]{1,0:T(8,128)S(1)}, f32[1024,128]{1,0:T(8,128)S(1)}) custom-call(bf16[1024,1408]{1,0:T(8,128)(2,1)} %bitcast.20.v, f32[1024,8]{1,0:T(8,128)S(1)} %pad_convert_fusion.masks, f32[8,1280]{1,0:T(8,128)S(1)} %pad_maximum_fusion.1.wb, f32[8,128]{1,0:T(8,128)S(1)} %pad.39.hp, ...), custom_call_target="tpu_custom_call" | custom-call | flops 536870912 | bytes 4194304 | tf_op jit(solution)/shard_map/prompt_state/pallas_call | solution.py:630
  135.9 0.8 copy-done.5
  136.8 0.8 copy-done.7
  137.6 9.9 %all-to-all-start.2 = ((bf16[4,256,1024]{2,1,0:T(8,128)(2,1)}), bf16[4,256,1024]{2,1,0:T(8,128)(2,1)S(1)}, u32[]{:S(2)}, u32[]{:S(2)}) async-start(bf16[4,256,1024]{2,1,0:T(8,128)(2,1)} %add_pairs.1.earlier_out), calls=%async_computation.2 | async-start | bytes 4194304 | tf_op jit(solution)/shard_map/all_to_all | solution.py:772
  147.5 1.0 copy-done.3
  148.5 1.0 copy-done.10
  149.5 0.9 copy-done.18
  150.5 0.9 copy-done.29
  152.1 0.9 copy-done.38
  153.1 33.6 %resp_mid.3 = (f32[8,4096]{1,0:T(8,128)S(1)}, f32[8,512]{1,0:T(8,128)S(1)}, f32[256,512]{1,0:T(8,128)S(1)}, f32[256,128]{1,0:T(8,128)S(1)}, f32[256,128]{1,0:T(8,128)S(1)}) custom-call(s32[1,1]{1,0:T(1,128)S(6)} %copy.52.len_ref, bf16[256,10240]{1,0:T(8,128)(2,1)} %bitcast.46, bf16[256,10240]{1,0:T(8,128)(2,1)} %bitcast.47, ...), custom_call_target="tpu_custom_call" | custom-call | flops 17179869184 | bytes 6291456 | tf_op jit(solution)/shard_map/resp_mid/pallas_call | solution.py:510
  190.1 1.5 reshape_squeeze.8
  191.5 1.5 reduce_sum.72
  194.9 1.3 constant_dynamic-update-slice_fusion.1
  196.3 2.3 pad_maximum_fusion.dc
  198.5 20.9 %all-to-all-done.2.states = bf16[4,256,1024]{2,1,0:T(8,128)(2,1)S(1)} async-done(((bf16[4,256,1024]{2,1,0:T(8,128)(2,1)}), bf16[4,256,1024]{2,1,0:T(8,128)(2,1)S(1)}, u32[]{:S(2)}, u32[]{:S(2)}) %all-to-all-start.2) | async-done | bytes 2097184 | tf_op jit(solution)/shard_map/all_to_all | solution.py:772
  219.5 1.0 copy-done.6
  220.5 1.0 copy-done.8
  221.6 0.8 copy-done.14
  223.0 27.4 %prompt_grad.1 = (f32[8,1280]{1,0:T(8,128)S(1)}, f32[8,128]{1,0:T(8,128)S(1)}) custom-call(bf16[1024,1408]{1,0:T(8,128)(2,1)} %bitcast.20.v, f32[1024,8]{1,0:T(8,128)S(1)} %pad_convert_fusion.masks, f32[8,1280]{1,0:T(8,128)S(1)} %copy-done.14, f32[8,128]{1,0:T(8,128)S(1)} %copy-done.33, f32[1024,128]{1,0:T(8,128)S(1)} %copy-done.6, ...), custom_call_target="tpu_custom_call" | custom-call | flops 1073741824 | bytes 8388608 | tf_op jit(solution)/shard_map/prompt_grad/pallas_call | solution.py:651
  250.5 1.2 copy-done
  251.7 1.0 copy-done.4
  252.7 0.9 copy-done.19
  253.7 0.9 copy-done.21
  254.6 0.9 copy-done.23
  255.5 0.9 copy-done.25
  256.4 0.9 copy-done.27
  257.3 8.7 %resp_end.1 = (f32[8,1024]{1,0:T(8,128)S(1)}, f32[8,128]{1,0:T(8,128)S(1)}) custom-call(bf16[256,10240]{1,0:T(8,128)(2,1)} %bitcast.48, f32[8,10240]{1,0:T(8,128)S(1)} %pad_convert_fusion.1.tail_c.tail_x.tail_b, f32[8,10240]{1,0:T(8,128)S(1)} %select_maximum_fusion.wb_c.wb_x.wb_b, bf16[256,1024]{1,0:T(8,128)(2,1)S(1)} %copy-done.4, ...), custom_call_target="tpu_custom_call" | custom-call | flops 2147483648 | bytes 12582912 | tf_op jit(solution)/shard_map/resp_end/pallas_call | solution.py:578
  266.6 1.0 slice_multiply_fusion
  268.1 15.3 %all_to_all.25 = f32[32,13,128]{2,1,0:T(8,128)S(1)} all-to-all(f32[32,13,128]{2,1,0:T(8,128)S(1)} %reshape.131), channel_id=1, replica_groups=mesh['group'=4,'resp'=8] {'group','resp'}, dimensions={0} | all-to-all | bytes 425984 | tf_op jit(solution)/shard_map/all_to_all | solution.py:695
  283.5 12.8 %all_to_all.26 = f32[32,13,128]{2,1,0:T(8,128)S(1)} all-to-all(f32[32,13,128]{2,1,0:T(8,128)S(1)} %broadcast_in_dim.44), channel_id=1, replica_groups=mesh['group'=4,'resp'=8] {'group','resp'}, dimensions={0} | all-to-all | bytes 425984 | tf_op jit(solution)/shard_map/all_to_all | solution.py:687
  (134 shorter events, 15.3 us)
Async XLA Ops:
  10.1 10.2 %copy-start.44 = (s32[1,4]{1,0:T(1,128)S(1)}, s32[1,4]{1,0:T(1,128)}, u32[]{:S(2)}) copy-start(s32[1,4]{1,0:T(1,128)} %param.13) | copy-start | bytes 52
  10.1 10.9 %copy-start.41 = (bf16[1,128,128]{2,1,0:T(8,128)(2,1)S(1)}, bf16[1,128,128]{2,1,0:T(8,128)(2,1)}, u32[]{:S(2)}) copy-start(bf16[1,128,128]{2,1,0:T(8,128)(2,1)} %param.12) | copy-start | bytes 98308
  10.1 22.0 %all-to-all-start = ((bf16[8,256,128]{2,1,0:T(8,128)(2,1)}), bf16[8,256,128]{2,1,0:T(8,128)(2,1)}, u32[]{:S(2)}, u32[]{:S(2)}) async-start(bf16[8,256,128]{2,1,0:T(8,128)(2,1)} %broadcast_in_dim.19), calls=%async_computation | async-start | bytes 1048576 | tf_op jit(solution)/shard_map/all_to_all | solution.py:687
  26.7 9.9 %copy-start.42 = (f32[3,128]{1,0:T(4,128)S(1)}, f32[3,128]{1,0:T(4,128)}, u32[]{:S(2)}) copy-start(f32[3,128]{1,0:T(4,128)} %param.21) | copy-start | bytes 4612
  26.7 10.7 %copy-start.15 = (bf16[1,1,256,128]{3,2,1,0:T(8,128)(2,1)S(1)}, bf16[1,1,256,128]{3,2,1,0:T(8,128)(2,1)}, u32[]{:S(2)}) copy-start(bf16[1,1,256,128]{3,2,1,0:T(8,128)(2,1)} %param.15) | copy-start | bytes 196612
  26.7 11.3 %copy-start.39 = (f32[4,10240]{1,0:T(4,128)S(1)}, f32[4,10240]{1,0:T(4,128)}, u32[]{:S(2)}) copy-start(f32[4,10240]{1,0:T(4,128)} %param.19) | copy-start | bytes 491524
  26.7 11.3 %copy-start.40 = (f32[10240]{0:T(1024)S(1)}, f32[10240]{0:T(1024)}, u32[]{:S(2)}) copy-start(f32[10240]{0:T(1024)} %param.20) | copy-start | bytes 122884
  32.1 87.7 %all-to-all-start.1 = ((bf16[8,128,1408]{2,1,0:T(8,128)(2,1)}), bf16[8,128,1408]{2,1,0:T(8,128)(2,1)}, u32[]{:S(2)}, u32[]{:S(2)}) async-start(bf16[8,128,1408]{2,1,0:T(8,128)(2,1)} %fusion.1), calls=%async_computation.1 | async-start | bytes 5767168 | tf_op jit(solution)/shard_map/all_to_all | solution.py:738
  36.5 213.9 %all-gather.3.cloned.1.call-start = ((), (), s32[]{:S(2)}) async-start(), calls=%async_computation.5 | async-start | bytes 4718592 | tf_op jit(solution)/shard_map/all_gather | solution.py:777
  37.3 3.6 %copy-start.30 = (f32[8,128]{1,0:T(8,128)}, f32[8,128]{1,0:T(8,128)S(1)}, u32[]{:S(2)}) copy-start(f32[8,128]{1,0:T(8,128)S(1)} %pad.36.hp) | copy-start | bytes 12292
  37.9 18.3 %copy-start.17 = (f32[256,128]{1,0:T(8,128)}, f32[256,128]{1,0:T(8,128)S(1)}, u32[]{:S(2)}) copy-start(f32[256,128]{1,0:T(8,128)S(1)} %get-tuple-element.33.step) | copy-start | bytes 393220
  38.0 18.3 %copy-start.28 = (f32[256,128]{1,0:T(8,128)}, f32[256,128]{1,0:T(8,128)S(1)}, u32[]{:S(2)}) copy-start(f32[256,128]{1,0:T(8,128)S(1)} %get-tuple-element.34.cum) | copy-start | bytes 393220
  38.0 18.3 %copy-start.37 = (f32[128,256]{1,0:T(8,128)}, f32[128,256]{1,0:T(8,128)S(1)}, u32[]{:S(2)}) copy-start(f32[128,256]{1,0:T(8,128)S(1)} %get-tuple-element.35) | copy-start | bytes 393220
  52.1 1.3 copy-start.1
  53.4 36.6 %copy-start.2 = (bf16[256,1024]{1,0:T(8,128)(2,1)}, bf16[256,1024]{1,0:T(8,128)(2,1)S(1)}, u32[]{:S(2)}) copy-start(bf16[256,1024]{1,0:T(8,128)(2,1)S(1)} %get-tuple-element.32.c_act) | copy-start | bytes 1572868
  53.4 62.0 %collective-permute-start = (bf16[4,256,1024]{2,1,0:T(8,128)(2,1)}, bf16[4,256,1024]{2,1,0:T(8,128)(2,1)}, u32[]{:S(2)}, u32[]{:S(2)}) collective-permute-start(bf16[4,256,1024]{2,1,0:T(8,128)(2,1)} %get-tuple-element.43), channel_id=1, source_target_pairs={{0,1},{1,0},{2,3},{3,2},{4,5},{5,4},{6,7},{7,6},{8,9},{9,8},{10,11... | collective-permute-start | bytes 6291464 | tf_op jit(solution)/shard_map/ppermute | solution.py:759
  55.3 64.4 %copy-start.32 = (f32[8,128]{1,0:T(8,128)}, f32[8,128]{1,0:T(8,128)S(1)}, u32[]{:S(2)}) copy-start(f32[8,128]{1,0:T(8,128)S(1)} %pad.39.hp) | copy-start | bytes 12292
  55.5 34.5 %copy-start.34 = (f32[1,8192]{1,0:T(1,128)}, f32[1,8192]{1,0:T(1,128)S(1)}, u32[]{:S(2)}) copy-start(f32[1,8192]{1,0:T(1,128)S(1)} %broadcast_in_dim_reshape.3.skip) | copy-start | bytes 98308
  56.1 33.9 %copy-start.9 = (f32[256,4,32]{2,0,1:T(8,128)}, f32[256,4,32]{2,0,1:T(8,128)S(1)}, u32[]{:S(2)}) copy-start(f32[256,4,32]{2,0,1:T(8,128)S(1)} %copy.39) | copy-start | bytes 393220
  56.2 63.5 %copy-start.13 = (f32[8,1280]{1,0:T(8,128)}, f32[8,1280]{1,0:T(8,128)S(1)}, u32[]{:S(2)}) copy-start(f32[8,1280]{1,0:T(8,128)S(1)} %pad_maximum_fusion.1.wb) | copy-start | bytes 122884
  90.0 0.8 copy-start.11
  90.8 0.7 copy-start.20
  135.9 0.8 copy-start.5
  136.7 0.8 copy-start.7
  137.6 81.9 %all-to-all-start.2 = ((bf16[4,256,1024]{2,1,0:T(8,128)(2,1)}), bf16[4,256,1024]{2,1,0:T(8,128)(2,1)S(1)}, u32[]{:S(2)}, u32[]{:S(2)}) async-start(bf16[4,256,1024]{2,1,0:T(8,128)(2,1)} %add_pairs.1.earlier_out), calls=%async_computation.2 | async-start | bytes 4194304 | tf_op jit(solution)/shard_map/all_to_all | solution.py:772
  147.5 1.0 copy-start.3
  148.5 1.0 copy-start.10
  149.5 0.9 copy-start.18
  150.5 0.9 copy-start.29
  151.4 0.8 copy-start.35
  152.1 0.9 copy-start.38
  186.7 0.8 copy-start.12
  187.5 0.7 copy-start.24
  188.2 0.6 copy-start.26
  219.5 1.0 copy-start.6
  220.5 1.0 copy-start.8
  221.6 0.8 copy-start.14
  222.4 0.7 copy-start.33
  223.0 27.4 %copy-start.16 = (bf16[1,1,256,128]{3,2,1,0:T(8,128)(2,1)S(1)}, bf16[1,1,256,128]{3,2,1,0:T(8,128)(2,1)}, u32[]{:S(2)}) copy-start(bf16[1,1,256,128]{3,2,1,0:T(8,128)(2,1)} %param.15) | copy-start | bytes 196612
  223.0 27.4 %copy-start.31 = (f32[8,128]{1,0:T(8,128)S(1)}, f32[8,128]{1,0:T(8,128)}, u32[]{:S(2)}) copy-start(f32[8,128]{1,0:T(8,128)} %copy-done.30) | copy-start | bytes 12292
  250.5 1.2 copy-start
  251.7 1.0 copy-start.4
  252.7 0.9 copy-start.19
  253.6 0.9 copy-start.21
  254.6 0.9 copy-start.23
  255.5 0.9 copy-start.25
  256.4 0.9 copy-start.27
  257.3 10.5 %copy-start.43 = (f32[128]{0:T(128)S(1)}, f32[128]{0:T(128)}, u32[]{:S(2)}) copy-start(f32[128]{0:T(128)} %reduce_sum.72) | copy-start | bytes 1540
  (2 other events, 1.2 us)
Sparse Core Ops, SparseCore 0:
  137.7 109.7 all-gather.2
